TPU v7x, 32 devices: a whole 2x2x4 slice. The times are simulated.
32 devices in a mesh: run: 2 (over y), tile: 4 (over z), sub: 2 (over x), pair: 2 (over core).
Axes of the slice: x: 2, y: 2, z: 4, core: 2. Of those that a mesh axis runs over, the one named last changes fastest.
Arguments:
- induction_vector: float32 [3, 4, 32, 512], P(None, ('run', 'pair'), ('tile', 'sub')), parts along dimension 1, may hold values from -6 to 6
- ohmic_spreading_number: float32 [4, 32, 512], P(('run', 'pair'), ('tile', 'sub')), parts along dimension 0, may hold values from 0.03 to 0.15
- reciprocal_surface: float32 [4, 32, 512], P(('run', 'pair'), ('tile', 'sub')), parts along dimension 0, may hold values from 0.5 to 2
- number_per_volume: float32 [4, 32, 512], P(('run', 'pair'), ('tile', 'sub')), parts along dimension 0, may hold values from 0.2 to 2
- thermal_kelvin: float32 [4, 32, 512], P(('run', 'pair'), ('tile', 'sub')), parts along dimension 0, may hold values from 0.5 to 4
- mapped_brick_members: int32 [4, 8, 8, 512], P(('run', 'pair'), ('tile', 'sub')), parts along dimension 0, may hold values from -1 to 2047, as said below
- arrival_owner_map: int32 [4, 8, 8, 512], P(('run', 'pair'), ('tile', 'sub')), parts along dimension 0, may hold values from 0 to 1023
- pedersen_sheet: float32 [64, 16, 512], P(('run', 'pair'), ('tile', 'sub')), parts along dimension 0, as said below
- electric_decay_rate: float32 [32, 512], P(('run', 'tile', 'sub')), parts along dimension 0, may hold values from 0.2 to 4
Outputs:
- advanced_field: float32 [3, 4, 32, 512], P(None, ('run', 'pair'), ('tile', 'sub')), parts along dimension 1
- boundary: float32 [2, 4, 32, 512], P(None, ('run', 'pair'), ('tile', 'sub')), parts along dimension 1
- potential: float32 [32, 512], P(('run', 'tile', 'sub')), parts along dimension 0
There are 2 independent parts, one for each index of `run`. A program takes and returns all parts, laid end to end along the dimension named above; each array names one. Nothing has to cross between parts.
Inputs may be any that keep to these rules, and one draw needn't show every extreme that they name: mapped_brick_members[p, s, d] lists cells of brick (p, s) whose field lines land on device d, -1 in empty slots; no cell appears twice among one brick's lists; in each run one device d receives exactly 512 cells from every brick. `pedersen_sheet`: positive.
All inputs are finite; a program needn't handle non-finite values.
Results may differ from a plain program's by a relative error of at most 0.00002.
Values sent between devices are 32-bit elements; how exact they have to be, the bound alone decides.
No kernel may reach another device: no remote copies, remote signals or barrier semaphores. Data moves between devices by JAX's collectives and lax.ppermute only.
A program may use at most 64 MiB of HBM per device.

v0:
```python
import jax
import jax.numpy as jnp
from jax import lax
from jax.sharding import PartitionSpec as P

DIFF_STEPS = 4
SWEEPS = 8


def extended(cells, sides, width):
    for axis, dim in sides:
        count = lax.axis_size(axis)
        ends = count - 1
        head = lax.slice_in_dim(cells, 0, width, axis=dim)
        tail = lax.slice_in_dim(cells, cells.shape[dim] - width, cells.shape[dim], axis=dim)
        cells = jnp.concatenate(
            [
                lax.ppermute(tail, axis, [(i, (i + 1) % count) for i in range(ends)]),
                cells,
                lax.ppermute(head, axis, [((i + 1) % count, i) for i in range(ends)]),
            ],
            axis=dim,
        )
    return cells


def extend_cells(current_state):
    return extended(current_state, ((("tile", "sub"), 2), ("pair", 1)), 1)


def extend_columns(grid_values):
    return extended(grid_values, ((("tile", "sub"), 0),), 1)


def advance_field(current_state, padded, ohmic_spreading_number):
    neighbours = (
        padded[:, 2:, 1:-1] + padded[:, :-2, 1:-1] + padded[:, 1:-1, 2:] + padded[:, 1:-1, :-2]
    )
    neighbours = neighbours + jnp.roll(current_state, -1, 3) + jnp.roll(current_state, 1, 3)
    return current_state + ohmic_spreading_number * (neighbours - 6.0 * current_state)


def local(
    induction_vector,
    ohmic_spreading_number,
    reciprocal_surface,
    number_per_volume,
    thermal_kelvin,
    mapped_brick_members,
    arrival_owner_map,
    pedersen_sheet,
    electric_decay_rate,
):
    padded = extend_cells(induction_vector)
    theta_diff = padded[2, 1:-1, 2:] - padded[2, 1:-1, :-2]
    phi_diff = jnp.roll(induction_vector[1], -1, 2) - jnp.roll(induction_vector[1], 1, 2)
    current = 0.5 * reciprocal_surface * (theta_diff - phi_diff)
    precipitation_power = 0.25 * number_per_volume * jnp.sqrt(thermal_kelvin)
    cell_lists = mapped_brick_members[0, 0]
    is_listed = cell_lists >= 0
    safe_index = jnp.where(is_listed, cell_lists, 0)
    sources = jnp.stack([current.reshape(-1), precipitation_power.reshape(-1)])
    payload = jnp.where(is_listed[None], sources[:, safe_index], 0.0)
    arrived = lax.all_to_all(payload, ("tile", "sub"), split_axis=1, concat_axis=1, tiled=True)
    land_columns = arrival_owner_map[0, 0]
    lat_rows, lon_cells = electric_decay_rate.shape
    column_count = lat_rows * lon_cells
    column_terms = (
        jnp.zeros((2, column_count), jnp.float32)
        .at[:, land_columns.reshape(-1)]
        .add(arrived.reshape(2, -1))
    )
    local_conductance = jnp.sum(pedersen_sheet, axis=0) + column_terms[1].reshape(
        lat_rows, lon_cells
    )
    aligned_current, conductance = lax.psum(
        (column_terms[0].reshape(lat_rows, lon_cells), local_conductance), "pair"
    )
    advanced = advance_field(induction_vector, padded, ohmic_spreading_number)
    for step_index in range(1, DIFF_STEPS):
        advanced = advance_field(advanced, extend_cells(advanced), ohmic_spreading_number)
    cond_rim = extend_columns(conductance)
    north_face = 0.5 * (conductance + cond_rim[:-2])
    south_face = 0.5 * (conductance + cond_rim[2:])
    east_face = 0.5 * (conductance + jnp.roll(conductance, -1, 1))
    west_face = 0.5 * (conductance + jnp.roll(conductance, 1, 1))
    diagonal = electric_decay_rate + north_face + south_face + east_face + west_face
    potential = aligned_current / diagonal
    for sweep_index in range(SWEEPS - 1):
        potential_rim = extend_columns(potential)
        potential = (
            aligned_current
            + north_face * potential_rim[:-2]
            + south_face * potential_rim[2:]
            + east_face * jnp.roll(potential, -1, 1)
            + west_face * jnp.roll(potential, 1, 1)
        ) / diagonal
    column_values = jnp.stack([potential, conductance]).reshape(2, -1)
    returned = lax.all_to_all(
        column_values[:, land_columns], ("tile", "sub"), split_axis=1, concat_axis=1, tiled=True
    )
    cell_count = current.size
    target = jnp.where(is_listed, cell_lists, cell_count)
    boundary = jnp.zeros((2, cell_count), jnp.float32).at[:, target].add(returned, mode="drop")
    boundary = boundary.reshape((2,) + current.shape)
    return (advanced, boundary, potential)


def solution(mesh):
    in_specs = (
        P(None, ("run", "pair"), ("tile", "sub"), None),
        P(("run", "pair"), ("tile", "sub"), None),
        P(("run", "pair"), ("tile", "sub"), None),
        P(("run", "pair"), ("tile", "sub"), None),
        P(("run", "pair"), ("tile", "sub"), None),
        P(("run", "pair"), ("tile", "sub"), None, None),
        P(("run", "pair"), ("tile", "sub"), None, None),
        P(("run", "pair"), ("tile", "sub"), None),
        P(("run", "tile", "sub"), None),
    )
    out_specs = (
        P(None, ("run", "pair"), ("tile", "sub"), None),
        P(None, ("run", "pair"), ("tile", "sub"), None),
        P(("run", "tile", "sub"), None),
    )
    return jax.shard_map(local, mesh=mesh, in_specs=in_specs, out_specs=out_specs, check_vma=False)
```

profile of v0, /device:TPU:12, one launch (start us, length us, event | category | flops | bytes accessed | tf_op | source)
XLA Modules:
  0.0 222.1 jit_solution(6610798430412156615)
XLA Ops:
  1.5 3.4 %collective-permute-start = (f32[3,1,1,512]{3,2,1,0:T(1,128)S(1)}, f32[3,1,1,512]{3,2,1,0:T(1,128)S(1)}, u32[]{:S(2)}, u32[]{:S(2)}) collective-permute-start(f32[3,1,1,512]{3,2,1,0:T(1,128)S(1)} %get-tuple-element.47), channel_id=1, source_target_pairs={{0,2},{2,4},{4,6},{6,8},{8,10},{10,12},{12,14},{1,3},{3,5},{5,7},{... | collective-permute-start | bytes 18440 | tf_op jit(solution)/shard_map/ppermute | solution.py:18
  4.9 3.3 %collective-permute-start.1 = (f32[3,1,1,512]{3,2,1,0:T(1,128)S(1)}, f32[3,1,1,512]{3,2,1,0:T(1,128)S(1)}, u32[]{:S(2)}, u32[]{:S(2)}) collective-permute-start(f32[3,1,1,512]{3,2,1,0:T(1,128)S(1)} %get-tuple-element.46), channel_id=1, source_target_pairs={{2,0},{4,2},{6,4},{8,6},{10,8},{12,10},{14,12},{3,1},{5,3},{7,5},{... | collective-permute-start | bytes 18440 | tf_op jit(solution)/shard_map/ppermute | solution.py:20
  21.8 10.8 %gather_fusion = f32[4096,2]{1,0:T(8,128)S(1)} fusion(f32[2,2048]{0,1:T(8,128)S(1)} %copy.23, s32[4096]{0:T(1024)S(1)} %broadcast_clamp_fusion.1), kind=kCustom, calls=%fused_computation | custom fusion | bytes 81920 | tf_op jit(solution)/shard_map/gather | solution.py:63
  33.8 5.3 %all-to-all-start = ((f32[2,8,512]{2,0,1:T(2,128)}), f32[2,8,512]{2,0,1:T(2,128)S(1)}, u32[]{:S(2)}, u32[]{:S(2)}) async-start(f32[2,8,512]{2,0,1:T(2,128)} %select_bitcast_fusion), calls=%async_computation | async-start | bytes 65536 | tf_op jit(solution)/shard_map/all_to_all | solution.py:64
  39.4 3.4 %collective-permute-start.4 = (f32[3,1,1,512]{3,2,1,0:T(1,128)S(1)}, f32[3,1,1,512]{3,2,1,0:T(1,128)S(1)}, u32[]{:S(2)}, u32[]{:S(2)}) collective-permute-start(f32[3,1,1,512]{3,2,1,0:T(1,128)S(1)} %get-tuple-element.41), channel_id=1, source_target_pairs={{0,2},{2,4},{4,6},{6,8},{8,10},{10,12},{12,14},{1,3},{3,5},{5,7},{... | collective-permute-start | bytes 18440 | tf_op jit(solution)/shard_map/ppermute | solution.py:18
  42.8 3.4 %collective-permute-start.5 = (f32[3,1,1,512]{3,2,1,0:T(1,128)S(1)}, f32[3,1,1,512]{3,2,1,0:T(1,128)S(1)}, u32[]{:S(2)}, u32[]{:S(2)}) collective-permute-start(f32[3,1,1,512]{3,2,1,0:T(1,128)S(1)} %get-tuple-element.40), channel_id=1, source_target_pairs={{2,0},{4,2},{6,4},{8,6},{10,8},{12,10},{14,12},{3,1},{5,3},{7,5},{... | collective-permute-start | bytes 18440 | tf_op jit(solution)/shard_map/ppermute | solution.py:20
  49.6 3.0 %collective-permute-start.7 = (f32[3,1,6,512]{3,2,1,0:T(8,128)S(1)}, f32[3,1,6,512]{3,2,1,0:T(8,128)S(1)}, u32[]{:S(2)}, u32[]{:S(2)}) collective-permute-start(f32[3,1,6,512]{3,2,1,0:T(8,128)S(1)} %pad_maximum_fusion.1), channel_id=1, source_target_pairs={{0,1},{2,3},{4,5},{6,7},{8,9},{10,11},{12,13},{14,15},{16,17},{18,... | collective-permute-start | bytes 110600 | tf_op jit(solution)/shard_map/ppermute | solution.py:18
  53.3 22.5 %scatter_custom_fusion = f32[2,1024]{0,1:T(8,128)S(1)} fusion(s32[4096]{0:T(1024)S(1)} %bitcast.76, f32[4096,2]{1,0:T(8,128)S(1)} %copy.25, f32[]{:T(128)} %constant.8.clone.1), kind=kCustom, calls=%fused_computation.8 | custom fusion | flops 8192 | bytes 8196 | tf_op jit(solution)/shard_map/scatter-add | solution.py:71
  78.9 4.3 %collective-permute-start.16 = (f32[1,512]{1,0:T(1,128)S(1)}, f32[1,512]{1,0:T(1,128)S(1)}, u32[]{:S(2)}, u32[]{:S(2)}) collective-permute-start(f32[1,512]{1,0:T(1,128)S(1)} %get-tuple-element.97), channel_id=1, source_target_pairs={{0,2},{2,4},{4,6},{6,8},{8,10},{10,12},{12,14},{1,3},{3,5},{5,7},{... | collective-permute-start | bytes 6152 | tf_op jit(solution)/shard_map/ppermute | solution.py:18
  88.8 3.4 %collective-permute-start.18 = (f32[1,512]{1,0:T(1,128)S(1)}, f32[1,512]{1,0:T(1,128)S(1)}, u32[]{:S(2)}, u32[]{:S(2)}) collective-permute-start(f32[1,512]{1,0:T(1,128)S(1)} %get-tuple-element.94), channel_id=1, source_target_pairs={{0,2},{2,4},{4,6},{6,8},{8,10},{10,12},{12,14},{1,3},{3,5},{5,7},{... | collective-permute-start | bytes 6152 | tf_op jit(solution)/shard_map/ppermute | solution.py:18
  92.2 3.4 %collective-permute-start.19 = (f32[1,512]{1,0:T(1,128)S(1)}, f32[1,512]{1,0:T(1,128)S(1)}, u32[]{:S(2)}, u32[]{:S(2)}) collective-permute-start(f32[1,512]{1,0:T(1,128)S(1)} %get-tuple-element.95), channel_id=1, source_target_pairs={{2,0},{4,2},{6,4},{8,6},{10,8},{12,10},{14,12},{3,1},{5,3},{7,5},{... | collective-permute-start | bytes 6152 | tf_op jit(solution)/shard_map/ppermute | solution.py:20
  97.8 4.3 %collective-permute-start.20 = (f32[1,512]{1,0:T(1,128)S(1)}, f32[1,512]{1,0:T(1,128)S(1)}, u32[]{:S(2)}, u32[]{:S(2)}) collective-permute-start(f32[1,512]{1,0:T(1,128)S(1)} %get-tuple-element.88), channel_id=1, source_target_pairs={{0,2},{2,4},{4,6},{6,8},{8,10},{10,12},{12,14},{1,3},{3,5},{5,7},{... | collective-permute-start | bytes 6152 | tf_op jit(solution)/shard_map/ppermute | solution.py:18
  107.8 3.4 %collective-permute-start.22 = (f32[1,512]{1,0:T(1,128)S(1)}, f32[1,512]{1,0:T(1,128)S(1)}, u32[]{:S(2)}, u32[]{:S(2)}) collective-permute-start(f32[1,512]{1,0:T(1,128)S(1)} %get-tuple-element.82), channel_id=1, source_target_pairs={{0,2},{2,4},{4,6},{6,8},{8,10},{10,12},{12,14},{1,3},{3,5},{5,7},{... | collective-permute-start | bytes 6152 | tf_op jit(solution)/shard_map/ppermute | solution.py:18
  111.1 3.4 %collective-permute-start.23 = (f32[1,512]{1,0:T(1,128)S(1)}, f32[1,512]{1,0:T(1,128)S(1)}, u32[]{:S(2)}, u32[]{:S(2)}) collective-permute-start(f32[1,512]{1,0:T(1,128)S(1)} %get-tuple-element.83), channel_id=1, source_target_pairs={{2,0},{4,2},{6,4},{8,6},{10,8},{12,10},{14,12},{3,1},{5,3},{7,5},{... | collective-permute-start | bytes 6152 | tf_op jit(solution)/shard_map/ppermute | solution.py:20
  119.6 3.9 %collective-permute-start.25 = (f32[1,512]{1,0:T(1,128)S(1)}, f32[1,512]{1,0:T(1,128)S(1)}, u32[]{:S(2)}, u32[]{:S(2)}) collective-permute-start(f32[1,512]{1,0:T(1,128)S(1)} %get-tuple-element.77), channel_id=1, source_target_pairs={{2,0},{4,2},{6,4},{8,6},{10,8},{12,10},{14,12},{3,1},{5,3},{7,5},{... | collective-permute-start | bytes 6152 | tf_op jit(solution)/shard_map/ppermute | solution.py:20
  128.0 3.9 %collective-permute-start.27 = (f32[1,512]{1,0:T(1,128)S(1)}, f32[1,512]{1,0:T(1,128)S(1)}, u32[]{:S(2)}, u32[]{:S(2)}) collective-permute-start(f32[1,512]{1,0:T(1,128)S(1)} %get-tuple-element.71), channel_id=1, source_target_pairs={{2,0},{4,2},{6,4},{8,6},{10,8},{12,10},{14,12},{3,1},{5,3},{7,5},{... | collective-permute-start | bytes 6152 | tf_op jit(solution)/shard_map/ppermute | solution.py:20
  136.5 3.9 %collective-permute-start.29 = (f32[1,512]{1,0:T(1,128)S(1)}, f32[1,512]{1,0:T(1,128)S(1)}, u32[]{:S(2)}, u32[]{:S(2)}) collective-permute-start(f32[1,512]{1,0:T(1,128)S(1)} %get-tuple-element.65), channel_id=1, source_target_pairs={{2,0},{4,2},{6,4},{8,6},{10,8},{12,10},{14,12},{3,1},{5,3},{7,5},{... | collective-permute-start | bytes 6152 | tf_op jit(solution)/shard_map/ppermute | solution.py:20
  145.0 3.9 %collective-permute-start.31 = (f32[1,512]{1,0:T(1,128)S(1)}, f32[1,512]{1,0:T(1,128)S(1)}, u32[]{:S(2)}, u32[]{:S(2)}) collective-permute-start(f32[1,512]{1,0:T(1,128)S(1)} %get-tuple-element.59), channel_id=1, source_target_pairs={{2,0},{4,2},{6,4},{8,6},{10,8},{12,10},{14,12},{3,1},{5,3},{7,5},{... | collective-permute-start | bytes 6152 | tf_op jit(solution)/shard_map/ppermute | solution.py:20
  150.8 10.8 %gather_fusion.1 = f32[4096,2]{1,0:T(8,128)S(1)} fusion(f32[2,1024]{0,1:T(8,128)S(1)} %copy.26, s32[4096]{0:T(1024)S(1)} %broadcast_clamp_fusion), kind=kCustom, calls=%fused_computation.1 | custom fusion | bytes 81920 | tf_op jit(solution)/shard_map/gather | solution.py:100
  162.8 5.8 %all-to-all-start.1 = ((f32[2,8,512]{2,0,1:T(2,128)}), f32[2,8,512]{2,0,1:T(2,128)S(1)}, u32[]{:S(2)}, u32[]{:S(2)}) async-start(f32[2,8,512]{2,0,1:T(2,128)} %bitcast.12), calls=%async_computation.1 | async-start | bytes 65536 | tf_op jit(solution)/shard_map/all_to_all | solution.py:99
  168.7 3.4 %collective-permute-start.8 = (f32[3,1,1,512]{3,2,1,0:T(1,128)S(1)}, f32[3,1,1,512]{3,2,1,0:T(1,128)S(1)}, u32[]{:S(2)}, u32[]{:S(2)}) collective-permute-start(f32[3,1,1,512]{3,2,1,0:T(1,128)S(1)} %get-tuple-element.35), channel_id=1, source_target_pairs={{0,2},{2,4},{4,6},{6,8},{8,10},{10,12},{12,14},{1,3},{3,5},{5,7},{... | collective-permute-start | bytes 18440 | tf_op jit(solution)/shard_map/ppermute | solution.py:18
  172.1 3.4 %collective-permute-start.9 = (f32[3,1,1,512]{3,2,1,0:T(1,128)S(1)}, f32[3,1,1,512]{3,2,1,0:T(1,128)S(1)}, u32[]{:S(2)}, u32[]{:S(2)}) collective-permute-start(f32[3,1,1,512]{3,2,1,0:T(1,128)S(1)} %get-tuple-element.34), channel_id=1, source_target_pairs={{2,0},{4,2},{6,4},{8,6},{10,8},{12,10},{14,12},{3,1},{5,3},{7,5},{... | collective-permute-start | bytes 18440 | tf_op jit(solution)/shard_map/ppermute | solution.py:20
  183.0 4.3 %collective-permute-start.12 = (f32[3,1,1,512]{3,2,1,0:T(1,128)S(1)}, f32[3,1,1,512]{3,2,1,0:T(1,128)S(1)}, u32[]{:S(2)}, u32[]{:S(2)}) collective-permute-start(f32[3,1,1,512]{3,2,1,0:T(1,128)S(1)} %get-tuple-element.29), channel_id=1, source_target_pairs={{0,2},{2,4},{4,6},{6,8},{8,10},{10,12},{12,14},{1,3},{3,5},{5,7},{... | collective-permute-start | bytes 18440 | tf_op jit(solution)/shard_map/ppermute | solution.py:18
  197.9 22.6 %scatter_custom_fusion.1 = f32[2,2048]{0,1:T(8,128)S(1)} fusion(s32[4096]{0:T(1024)S(1)} %bitcast.75, f32[4096,2]{1,0:T(8,128)S(1)} %copy.28, f32[]{:T(128)} %constant.8.clone.1), kind=kCustom, calls=%fused_computation.6 | custom fusion | flops 8192 | bytes 16388 | tf_op jit(solution)/shard_map/scatter-add | solution.py:104
  (143 shorter events, 78.0 us)
Async XLA Ops:
  1.5 13.9 %collective-permute-start = (f32[3,1,1,512]{3,2,1,0:T(1,128)S(1)}, f32[3,1,1,512]{3,2,1,0:T(1,128)S(1)}, u32[]{:S(2)}, u32[]{:S(2)}) collective-permute-start(f32[3,1,1,512]{3,2,1,0:T(1,128)S(1)} %get-tuple-element.47), channel_id=1, source_target_pairs={{0,2},{2,4},{4,6},{6,8},{8,10},{10,12},{12,14},{1,3},{3,5},{5,7},{... | collective-permute-start | bytes 18440 | tf_op jit(solution)/shard_map/ppermute | solution.py:18
  4.9 10.5 %collective-permute-start.1 = (f32[3,1,1,512]{3,2,1,0:T(1,128)S(1)}, f32[3,1,1,512]{3,2,1,0:T(1,128)S(1)}, u32[]{:S(2)}, u32[]{:S(2)}) collective-permute-start(f32[3,1,1,512]{3,2,1,0:T(1,128)S(1)} %get-tuple-element.46), channel_id=1, source_target_pairs={{2,0},{4,2},{6,4},{8,6},{10,8},{12,10},{14,12},{3,1},{5,3},{7,5},{... | collective-permute-start | bytes 18440 | tf_op jit(solution)/shard_map/ppermute | solution.py:20
  16.1 23.0 %collective-permute-start.2 = (f32[3,1,6,512]{3,2,1,0:T(8,128)S(1)}, f32[3,1,6,512]{3,2,1,0:T(8,128)S(1)}, u32[]{:S(2)}, u32[]{:S(2)}) collective-permute-start(f32[3,1,6,512]{3,2,1,0:T(8,128)S(1)} %pad_maximum_fusion), channel_id=1, source_target_pairs={{1,0},{3,2},{5,4},{7,6},{9,8},{11,10},{13,12},{15,14},{17,16},{19,... | collective-permute-start | bytes 110600 | tf_op jit(solution)/shard_map/ppermute | solution.py:20
  17.4 21.7 %collective-permute-start.3 = (f32[3,1,6,512]{3,2,1,0:T(8,128)S(1)}, f32[3,1,6,512]{3,2,1,0:T(8,128)S(1)}, u32[]{:S(2)}, u32[]{:S(2)}) collective-permute-start(f32[3,1,6,512]{3,2,1,0:T(8,128)S(1)} %pad_maximum_fusion), channel_id=1, source_target_pairs={{0,1},{2,3},{4,5},{6,7},{8,9},{10,11},{12,13},{14,15},{16,17},{18,... | collective-permute-start | bytes 110600 | tf_op jit(solution)/shard_map/ppermute | solution.py:18
  33.8 18.8 %all-to-all-start = ((f32[2,8,512]{2,0,1:T(2,128)}), f32[2,8,512]{2,0,1:T(2,128)S(1)}, u32[]{:S(2)}, u32[]{:S(2)}) async-start(f32[2,8,512]{2,0,1:T(2,128)} %select_bitcast_fusion), calls=%async_computation | async-start | bytes 65536 | tf_op jit(solution)/shard_map/all_to_all | solution.py:64
  39.4 6.8 %collective-permute-start.4 = (f32[3,1,1,512]{3,2,1,0:T(1,128)S(1)}, f32[3,1,1,512]{3,2,1,0:T(1,128)S(1)}, u32[]{:S(2)}, u32[]{:S(2)}) collective-permute-start(f32[3,1,1,512]{3,2,1,0:T(1,128)S(1)} %get-tuple-element.41), channel_id=1, source_target_pairs={{0,2},{2,4},{4,6},{6,8},{8,10},{10,12},{12,14},{1,3},{3,5},{5,7},{... | collective-permute-start | bytes 18440 | tf_op jit(solution)/shard_map/ppermute | solution.py:18
  42.8 5.5 %collective-permute-start.5 = (f32[3,1,1,512]{3,2,1,0:T(1,128)S(1)}, f32[3,1,1,512]{3,2,1,0:T(1,128)S(1)}, u32[]{:S(2)}, u32[]{:S(2)}) collective-permute-start(f32[3,1,1,512]{3,2,1,0:T(1,128)S(1)} %get-tuple-element.40), channel_id=1, source_target_pairs={{2,0},{4,2},{6,4},{8,6},{10,8},{12,10},{14,12},{3,1},{5,3},{7,5},{... | collective-permute-start | bytes 18440 | tf_op jit(solution)/shard_map/ppermute | solution.py:20
  48.3 120.3 %collective-permute-start.6 = (f32[3,1,6,512]{3,2,1,0:T(8,128)S(1)}, f32[3,1,6,512]{3,2,1,0:T(8,128)S(1)}, u32[]{:S(2)}, u32[]{:S(2)}) collective-permute-start(f32[3,1,6,512]{3,2,1,0:T(8,128)S(1)} %pad_maximum_fusion.1), channel_id=1, source_target_pairs={{1,0},{3,2},{5,4},{7,6},{9,8},{11,10},{13,12},{15,14},{17,16},{19,... | collective-permute-start | bytes 110600 | tf_op jit(solution)/shard_map/ppermute | solution.py:20
  49.6 119.0 %collective-permute-start.7 = (f32[3,1,6,512]{3,2,1,0:T(8,128)S(1)}, f32[3,1,6,512]{3,2,1,0:T(8,128)S(1)}, u32[]{:S(2)}, u32[]{:S(2)}) collective-permute-start(f32[3,1,6,512]{3,2,1,0:T(8,128)S(1)} %pad_maximum_fusion.1), channel_id=1, source_target_pairs={{0,1},{2,3},{4,5},{6,7},{8,9},{10,11},{12,13},{14,15},{16,17},{18,... | collective-permute-start | bytes 110600 | tf_op jit(solution)/shard_map/ppermute | solution.py:18
  78.9 6.8 %collective-permute-start.16 = (f32[1,512]{1,0:T(1,128)S(1)}, f32[1,512]{1,0:T(1,128)S(1)}, u32[]{:S(2)}, u32[]{:S(2)}) collective-permute-start(f32[1,512]{1,0:T(1,128)S(1)} %get-tuple-element.97), channel_id=1, source_target_pairs={{0,2},{2,4},{4,6},{6,8},{8,10},{10,12},{12,14},{1,3},{3,5},{5,7},{... | collective-permute-start | bytes 6152 | tf_op jit(solution)/shard_map/ppermute | solution.py:18
  88.8 6.8 %collective-permute-start.18 = (f32[1,512]{1,0:T(1,128)S(1)}, f32[1,512]{1,0:T(1,128)S(1)}, u32[]{:S(2)}, u32[]{:S(2)}) collective-permute-start(f32[1,512]{1,0:T(1,128)S(1)} %get-tuple-element.94), channel_id=1, source_target_pairs={{0,2},{2,4},{4,6},{6,8},{8,10},{10,12},{12,14},{1,3},{3,5},{5,7},{... | collective-permute-start | bytes 6152 | tf_op jit(solution)/shard_map/ppermute | solution.py:18
  97.8 6.8 %collective-permute-start.20 = (f32[1,512]{1,0:T(1,128)S(1)}, f32[1,512]{1,0:T(1,128)S(1)}, u32[]{:S(2)}, u32[]{:S(2)}) collective-permute-start(f32[1,512]{1,0:T(1,128)S(1)} %get-tuple-element.88), channel_id=1, source_target_pairs={{0,2},{2,4},{4,6},{6,8},{8,10},{10,12},{12,14},{1,3},{3,5},{5,7},{... | collective-permute-start | bytes 6152 | tf_op jit(solution)/shard_map/ppermute | solution.py:18
  107.8 6.8 %collective-permute-start.22 = (f32[1,512]{1,0:T(1,128)S(1)}, f32[1,512]{1,0:T(1,128)S(1)}, u32[]{:S(2)}, u32[]{:S(2)}) collective-permute-start(f32[1,512]{1,0:T(1,128)S(1)} %get-tuple-element.82), channel_id=1, source_target_pairs={{0,2},{2,4},{4,6},{6,8},{8,10},{10,12},{12,14},{1,3},{3,5},{5,7},{... | collective-permute-start | bytes 6152 | tf_op jit(solution)/shard_map/ppermute | solution.py:18
  116.8 6.8 %collective-permute-start.24 = (f32[1,512]{1,0:T(1,128)S(1)}, f32[1,512]{1,0:T(1,128)S(1)}, u32[]{:S(2)}, u32[]{:S(2)}) collective-permute-start(f32[1,512]{1,0:T(1,128)S(1)} %get-tuple-element.76), channel_id=1, source_target_pairs={{0,2},{2,4},{4,6},{6,8},{8,10},{10,12},{12,14},{1,3},{3,5},{5,7},{... | collective-permute-start | bytes 6152 | tf_op jit(solution)/shard_map/ppermute | solution.py:18
  125.2 6.8 %collective-permute-start.26 = (f32[1,512]{1,0:T(1,128)S(1)}, f32[1,512]{1,0:T(1,128)S(1)}, u32[]{:S(2)}, u32[]{:S(2)}) collective-permute-start(f32[1,512]{1,0:T(1,128)S(1)} %get-tuple-element.70), channel_id=1, source_target_pairs={{0,2},{2,4},{4,6},{6,8},{8,10},{10,12},{12,14},{1,3},{3,5},{5,7},{... | collective-permute-start | bytes 6152 | tf_op jit(solution)/shard_map/ppermute | solution.py:18
  133.7 6.8 %collective-permute-start.28 = (f32[1,512]{1,0:T(1,128)S(1)}, f32[1,512]{1,0:T(1,128)S(1)}, u32[]{:S(2)}, u32[]{:S(2)}) collective-permute-start(f32[1,512]{1,0:T(1,128)S(1)} %get-tuple-element.64), channel_id=1, source_target_pairs={{0,2},{2,4},{4,6},{6,8},{8,10},{10,12},{12,14},{1,3},{3,5},{5,7},{... | collective-permute-start | bytes 6152 | tf_op jit(solution)/shard_map/ppermute | solution.py:18
  142.1 6.8 %collective-permute-start.30 = (f32[1,512]{1,0:T(1,128)S(1)}, f32[1,512]{1,0:T(1,128)S(1)}, u32[]{:S(2)}, u32[]{:S(2)}) collective-permute-start(f32[1,512]{1,0:T(1,128)S(1)} %get-tuple-element.58), channel_id=1, source_target_pairs={{0,2},{2,4},{4,6},{6,8},{8,10},{10,12},{12,14},{1,3},{3,5},{5,7},{... | collective-permute-start | bytes 6152 | tf_op jit(solution)/shard_map/ppermute | solution.py:18
  162.8 34.4 %all-to-all-start.1 = ((f32[2,8,512]{2,0,1:T(2,128)}), f32[2,8,512]{2,0,1:T(2,128)S(1)}, u32[]{:S(2)}, u32[]{:S(2)}) async-start(f32[2,8,512]{2,0,1:T(2,128)} %bitcast.12), calls=%async_computation.1 | async-start | bytes 65536 | tf_op jit(solution)/shard_map/all_to_all | solution.py:99
  168.7 6.8 %collective-permute-start.8 = (f32[3,1,1,512]{3,2,1,0:T(1,128)S(1)}, f32[3,1,1,512]{3,2,1,0:T(1,128)S(1)}, u32[]{:S(2)}, u32[]{:S(2)}) collective-permute-start(f32[3,1,1,512]{3,2,1,0:T(1,128)S(1)} %get-tuple-element.35), channel_id=1, source_target_pairs={{0,2},{2,4},{4,6},{6,8},{8,10},{10,12},{12,14},{1,3},{3,5},{5,7},{... | collective-permute-start | bytes 18440 | tf_op jit(solution)/shard_map/ppermute | solution.py:18
  172.1 5.5 %collective-permute-start.9 = (f32[3,1,1,512]{3,2,1,0:T(1,128)S(1)}, f32[3,1,1,512]{3,2,1,0:T(1,128)S(1)}, u32[]{:S(2)}, u32[]{:S(2)}) collective-permute-start(f32[3,1,1,512]{3,2,1,0:T(1,128)S(1)} %get-tuple-element.34), channel_id=1, source_target_pairs={{2,0},{4,2},{6,4},{8,6},{10,8},{12,10},{14,12},{3,1},{5,3},{7,5},{... | collective-permute-start | bytes 18440 | tf_op jit(solution)/shard_map/ppermute | solution.py:20
  183.0 6.8 %collective-permute-start.12 = (f32[3,1,1,512]{3,2,1,0:T(1,128)S(1)}, f32[3,1,1,512]{3,2,1,0:T(1,128)S(1)}, u32[]{:S(2)}, u32[]{:S(2)}) collective-permute-start(f32[3,1,1,512]{3,2,1,0:T(1,128)S(1)} %get-tuple-element.29), channel_id=1, source_target_pairs={{0,2},{2,4},{4,6},{6,8},{8,10},{10,12},{12,14},{1,3},{3,5},{5,7},{... | collective-permute-start | bytes 18440 | tf_op jit(solution)/shard_map/ppermute | solution.py:18
  187.2 5.5 %collective-permute-start.13 = (f32[3,1,1,512]{3,2,1,0:T(1,128)S(1)}, f32[3,1,1,512]{3,2,1,0:T(1,128)S(1)}, u32[]{:S(2)}, u32[]{:S(2)}) collective-permute-start(f32[3,1,1,512]{3,2,1,0:T(1,128)S(1)} %get-tuple-element.28), channel_id=1, source_target_pairs={{2,0},{4,2},{6,4},{8,6},{10,8},{12,10},{14,12},{3,1},{5,3},{7,5},{... | collective-permute-start | bytes 18440 | tf_op jit(solution)/shard_map/ppermute | solution.py:20
  192.8 28.6 %collective-permute-start.14 = (f32[3,1,6,512]{3,2,1,0:T(8,128)S(1)}, f32[3,1,6,512]{3,2,1,0:T(8,128)S(1)}, u32[]{:S(2)}, u32[]{:S(2)}) collective-permute-start(f32[3,1,6,512]{3,2,1,0:T(8,128)S(1)} %pad_maximum_fusion.3), channel_id=1, source_target_pairs={{1,0},{3,2},{5,4},{7,6},{9,8},{11,10},{13,12},{15,14},{17,16},{19,... | collective-permute-start | bytes 110600 | tf_op jit(solution)/shard_map/ppermute | solution.py:20
  194.1 27.3 %collective-permute-start.15 = (f32[3,1,6,512]{3,2,1,0:T(8,128)S(1)}, f32[3,1,6,512]{3,2,1,0:T(8,128)S(1)}, u32[]{:S(2)}, u32[]{:S(2)}) collective-permute-start(f32[3,1,6,512]{3,2,1,0:T(8,128)S(1)} %pad_maximum_fusion.3), channel_id=1, source_target_pairs={{0,1},{2,3},{4,5},{6,7},{8,9},{10,11},{12,13},{14,15},{16,17},{18,... | collective-permute-start | bytes 110600 | tf_op jit(solution)/shard_map/ppermute | solution.py:18
  (14 other events, 200.1 us)
where the time goes:
time: 225 us; the launch traced here: 222 us
  starting transfers between devices  109 us (48%)
  other arithmetic  52.9 us (24%)
  local copies, waits for them, and re-layouts  32.6 us (14%)
  waiting for transfers between devices  23.7 us (11%)
  blocking collectives  2.5 us (1%)
    ppermute x16, starting transfers between devices, extended(): lax.ppermute(tail, axis, [(i, (i + 1) % count) for i in range(ends)])  53 us
    ppermute x16, starting transfers between devices, extended(): lax.ppermute(head, axis, [((i + 1) % count, i) for i in range(ends)])  45.1 us
    ppermute x16, waiting for transfers between devices, extended(): lax.ppermute(head, axis, [((i + 1) % count, i) for i in range(ends)])  22.9 us
    scatter-add x1, other arithmetic, local(): jnp.zeros((2, cell_count), jnp.float32).at[:, target]  22.6 us
    scatter-add x1, other arithmetic, local(): column_terms = jnp.zeros((2, column_count), jnp.float32).at[:, land_colum...  22.5 us
    gather x2, local copies, waits for them, and re-layouts, local(): column_values[:, land_columns]  12 us
    gather x2, local copies, waits for them, and re-layouts, local(): payload = jnp.where(is_listed[None], sources[:, safe_index], 0.0)  11.4 us
    all_to_all x1, starting transfers between devices, local(): lax.all_to_all(column_values[:, land_columns], ('tile', 'sub'), split_axi...  5.8 us
  transfers between devices with their start and end apart: 34, of which 12 were waited for; matrix products, arithmetic and copies ran while one was open for 37% of the time, Pallas kernels for 0%

commit v1 on v0

--- a/solution.py
+++ b/solution.py
@@ -1,6 +1,10 @@
+import functools
+
 import jax
 import jax.numpy as jnp
 from jax import lax
+from jax.experimental import pallas as pl
+from jax.experimental.pallas import tpu as pltpu
 from jax.sharding import PartitionSpec as P
 
 DIFF_STEPS = 4
@@ -40,7 +44,7 @@
     return current_state + ohmic_spreading_number * (neighbours - 6.0 * current_state)
 
 
-def local(
+def stepwise(
     induction_vector,
     ohmic_spreading_number,
     reciprocal_surface,
@@ -106,6 +110,358 @@
     return (advanced, boundary, potential)
 
 
+LANES = 128
+PEERS = 8
+RING = ("tile", "sub")
+GROUP = ("tile", "sub", "pair")
+CURRENT, FLUX, RIM_WEIGHT, CELL, OWNER, FIRST_ROW, LAST_ROW, DECAY = range(8)
+CHUNK_FIELDS = 10
+
+
+def pick_lanes(row, lane):
+    return jnp.take_along_axis(
+        jnp.broadcast_to(row, lane.shape), lane, axis=1, mode="promise_in_bounds"
+    )
+
+
+def blocks_of(count):
+    return [slice(b * LANES, (b + 1) * LANES) for b in range(count)]
+
+
+def field_rows(field, block, blocks):
+    return pl.ds(field * blocks + block, PEERS, stride=CHUNK_FIELDS * blocks)
+
+
+def three_terms(values):
+    first = values.astype(jnp.bfloat16)
+    rest = values - first.astype(jnp.float32)
+    second = rest.astype(jnp.bfloat16)
+    third = (rest - second.astype(jnp.float32)).astype(jnp.bfloat16)
+    return first, second, third
+
+
+def one_hot_sums(rows, lanes, terms, row_count):
+    total = None
+    slots = rows.shape[1]
+    row_at = lax.broadcasted_iota(jnp.int32, (row_count, slots), 0)
+    lane_at = lax.broadcasted_iota(jnp.int32, (LANES, slots), 0)
+    for s in range(rows.shape[0]):
+        here = row_at == rows[s : s + 1]
+        left = jnp.concatenate(
+            [
+                jnp.where(here, jnp.broadcast_to(t[s : s + 1], here.shape), 0.0)
+                for t in terms
+            ],
+            axis=0,
+        ).astype(jnp.bfloat16)
+        right = jnp.where(lane_at == lanes[s : s + 1], 1.0, 0.0).astype(jnp.bfloat16)
+        part = lax.dot_general(
+            left, right, (((1,), (1,)), ((), ())), preferred_element_type=jnp.float32
+        )
+        total = part if total is None else total + part
+    return total
+
+
+def collect_kernel(field, reciprocal, number, kelvin, lists, owners, decay, sent, packet):
+    theta_rows, lon = reciprocal.shape[1:]
+    blocks = lon // LANES
+    toward_theta = field[2, 0]
+    toward_phi = field[1, 0]
+    zero_row = jnp.zeros((1, lon), jnp.float32)
+    half = 0.5 * reciprocal[0]
+    theta_diff = jnp.concatenate([toward_theta[1:], zero_row], 0) - jnp.concatenate(
+        [zero_row, toward_theta[:-1]], 0
+    )
+    phi_diff = pltpu.roll(toward_phi, lon - 1, 1) - pltpu.roll(toward_phi, 1, 1)
+    current = half * (theta_diff - phi_diff)
+    flux = 0.25 * number[0] * jnp.sqrt(kelvin[0])
+    for b, span in enumerate(blocks_of(blocks)):
+        cell = lists[:, span]
+        lane = cell & (LANES - 1)
+        row = cell >> 7
+        taken = [jnp.zeros(cell.shape, jnp.float32)] * 3
+        for theta in range(theta_rows):
+            for c, source in enumerate(blocks_of(blocks)):
+                here = row == theta * blocks + c
+                at = slice(theta, theta + 1)
+                tables = [current[at, source], flux[at, source]]
+                if theta == 0:
+                    tables.append(-half[at, source])
+                if theta == theta_rows - 1:
+                    tables.append(half[at, source])
+                for k, table in enumerate(tables):
+                    taken[k] = jnp.where(here, pick_lanes(table, lane), taken[k])
+        values = taken + [cell.astype(jnp.float32), owners[:, span].astype(jnp.float32)]
+        values += [
+            jnp.broadcast_to(r[:, span], cell.shape)
+            for r in (toward_theta[:1], toward_theta[-1:], decay[0:1], decay[1:2])
+        ]
+        values.append(jnp.zeros(cell.shape, jnp.float32))
+        for k, value in enumerate(values):
+            sent[field_rows(k, b, blocks), :] = value
+    for k in range(3):
+        packet[k * theta_rows : (k + 1) * theta_rows] = field[k, 0]
+
+
+def deposit_kernel(arrived, owners, sheet, sums):
+    lon = sheet.shape[-1]
+    blocks = lon // LANES
+    lat_rows = sheet.shape[1]
+    peer = lax.broadcasted_iota(jnp.int32, (PEERS, LANES), 0)
+    above, below = [], []
+    for b in range(blocks):
+        last = pltpu.roll(arrived[field_rows(LAST_ROW, b, blocks), :], 1, 0)
+        above.append(jnp.where(peer == 0, 0.0, last))
+        first = pltpu.roll(arrived[field_rows(FIRST_ROW, b, blocks), :], PEERS - 1, 0)
+        below.append(jnp.where(peer == PEERS - 1, 0.0, first))
+    currents, fluxes = [], []
+    for b in range(blocks):
+        cell = arrived[field_rows(CELL, b, blocks), :].astype(jnp.int32)
+        phi_block = (cell >> 7) & (blocks - 1)
+        lane = cell & (LANES - 1)
+        rim = jnp.zeros((PEERS, LANES), jnp.float32)
+        for c in range(blocks):
+            found = jnp.where(
+                cell < lon, pick_lanes(above[c], lane), pick_lanes(below[c], lane)
+            )
+            rim = jnp.where(phi_block == c, found, rim)
+        weight = arrived[field_rows(RIM_WEIGHT, b, blocks), :]
+        currents.append(arrived[field_rows(CURRENT, b, blocks), :] + weight * rim)
+        fluxes.append(arrived[field_rows(FLUX, b, blocks), :])
+    column = owners[...]
+    terms = three_terms(jnp.concatenate(currents, 1)) + three_terms(jnp.concatenate(fluxes, 1))
+    rows = lat_rows * blocks
+    total = one_hot_sums(
+        column >> 7, column & (LANES - 1), [t.astype(jnp.float32) for t in terms], rows
+    )
+    parts = [total[k * rows : (k + 1) * rows] for k in range(6)]
+    current = parts[0] + parts[1] + parts[2]
+    flux = parts[3] + parts[4] + parts[5]
+    level_sum = jnp.sum(sheet[...], axis=0)
+    level_rows = jnp.concatenate(
+        [level_sum[i : i + 1, span] for i in range(lat_rows) for span in blocks_of(blocks)], 0
+    )
+    both = jnp.concatenate([current, flux + level_rows], 0)
+    for k in range(sums.shape[0] // (2 * rows)):
+        sums[k * 2 * rows : (k + 1) * 2 * rows] = both
+
+
+def invert_kernel(arrived, lists, found, *, lat_rows):
+    lon = lists.shape[1]
+    blocks = lon // LANES
+    owner = jnp.concatenate(
+        [arrived[field_rows(OWNER, b, blocks), :] for b in range(blocks)], 1
+    ).astype(jnp.int32)
+    device = lax.broadcasted_iota(jnp.int32, owner.shape, 0)
+    row = (owner >> 7) + device * (lat_rows * blocks) + 1
+    lane = owner & (LANES - 1)
+    cell = lists[...]
+    cell_rows = found.shape[0] // 2
+    found[...] = one_hot_sums(
+        cell >> 7,
+        cell & (LANES - 1),
+        [row.astype(jnp.float32), lane.astype(jnp.float32)],
+        cell_rows,
+    ).astype(jnp.int32)
+
+
+def advance_kernel(own, other, even, odd, advanced, window):
+    theta_rows = advanced.shape[2]
+    span = 4 * theta_rows
+    is_odd = (lax.axis_index(RING) & 1) == 1
+    window[...] = jnp.zeros_like(window)
+    for shell, middle in enumerate((own, other)):
+        for k in range(4):
+            at = slice(k * theta_rows, (k + 1) * theta_rows)
+            far = slice(shell * span + k * theta_rows, shell * span + (k + 1) * theta_rows)
+            place = shell * 4 + k
+            after = jnp.where(is_odd, odd[far], even[far])
+            before = jnp.where(is_odd, even[far], odd[far])
+            window[place, 0:theta_rows] = before
+            window[place, theta_rows : 2 * theta_rows] = middle[at]
+            window[place, 2 * theta_rows : 3 * theta_rows] = after
+    rows, lon = window.shape[1:]
+    spreading = [window[3], window[7]]
+    for k in range(3):
+        state = [window[k], window[4 + k]]
+        for _ in range(DIFF_STEPS):
+            later = []
+            for shell in range(2):
+                here = state[shell]
+                around = state[1 - shell] + pltpu.roll(here, rows - 1, 0) + pltpu.roll(here, 1, 0)
+                around = around + pltpu.roll(here, lon - 1, 1) + pltpu.roll(here, 1, 1)
+                later.append(here + spreading[shell] * (around - 6.0 * here))
+            state = later
+        advanced[k, 0] = state[0][theta_rows : 2 * theta_rows]
+
+
+def solve_kernel(sums, arrived, found, boundary, potential):
+    lon = potential.shape[1]
+    blocks = lon // LANES
+    rows = 2 * blocks
+    ring = lax.broadcasted_iota(jnp.int32, (PEERS, lon), 0)
+
+    def summed(term, lat):
+        return jnp.concatenate(
+            [
+                sum(
+                    sums[pl.ds((pair * 2 + term) * rows + lat * blocks + b, PEERS, stride=4 * rows), :]
+                    for pair in range(2)
+                )
+                for b in range(blocks)
+            ],
+            1,
+        )
+
+    def decay_rows(lat):
+        return jnp.concatenate(
+            [arrived[field_rows(DECAY + lat, b, blocks), :] for b in range(blocks)], 1
+        )
+
+    def before(values):
+        return jnp.where(ring == 0, 0.0, pltpu.roll(values, 1, 0))
+
+    def after(values):
+        return jnp.where(ring == PEERS - 1, 0.0, pltpu.roll(values, PEERS - 1, 0))
+
+    def east(values):
+        return pltpu.roll(values, lon - 1, 1)
+
+    def west(values):
+        return pltpu.roll(values, 1, 1)
+
+    aligned = [summed(0, 0), summed(0, 1)]
+    conductance = [summed(1, 0), summed(1, 1)]
+    faces = []
+    middle = 0.5 * (conductance[0] + conductance[1])
+    north = (0.5 * (conductance[0] + before(conductance[1])), middle)
+    south = (middle, 0.5 * (conductance[1] + after(conductance[0])))
+    level = []
+    for lat in range(2):
+        here = conductance[lat]
+        east_face = 0.5 * (here + east(here))
+        west_face = 0.5 * (here + west(here))
+        diagonal = decay_rows(lat) + north[lat] + south[lat] + east_face + west_face
+        inverse = 1.0 / diagonal
+        faces.append([f * inverse for f in (north[lat], south[lat], east_face, west_face)])
+        aligned[lat] = aligned[lat] * inverse
+        level.append(aligned[lat])
+    for _ in range(SWEEPS - 1):
+        around = ((before(level[1]), level[1]), (level[0], after(level[0])))
+        level = [
+            aligned[lat]
+            + faces[lat][0] * around[lat][0]
+            + faces[lat][1] * around[lat][1]
+            + faces[lat][2] * east(level[lat])
+            + faces[lat][3] * west(level[lat])
+            for lat in range(2)
+        ]
+    me = lax.axis_index(RING)
+    for lat in range(2):
+        potential[lat : lat + 1] = jnp.sum(
+            jnp.where(ring == me, level[lat], 0.0), axis=0, keepdims=True
+        )
+    cell_rows = found.shape[0] // 2
+    lane = found[cell_rows:]
+    row = found[:cell_rows]
+    taken = [jnp.zeros(lane.shape, jnp.float32)] * 2
+    for device in range(PEERS):
+        for lat in range(2):
+            for b, span in enumerate(blocks_of(blocks)):
+                here = row == device * rows + lat * blocks + b + 1
+                for k, table in enumerate((level[lat], conductance[lat])):
+                    one = table[device : device + 1, span]
+                    taken[k] = jnp.where(here, pick_lanes(one, lane), taken[k])
+    for k in range(2):
+        for r in range(cell_rows):
+            boundary[k, 0, r // blocks : r // blocks + 1, blocks_of(blocks)[r % blocks]] = taken[k][
+                r : r + 1
+            ]
+
+
+def shape_of(*dims):
+    return jax.ShapeDtypeStruct(dims, jnp.float32)
+
+
+def short_plan(
+    induction_vector,
+    ohmic_spreading_number,
+    reciprocal_surface,
+    number_per_volume,
+    thermal_kelvin,
+    mapped_brick_members,
+    arrival_owner_map,
+    pedersen_sheet,
+    electric_decay_rate,
+):
+    lists = mapped_brick_members[0, 0]
+    owners = arrival_owner_map[0, 0]
+    lat_rows, lon = electric_decay_rate.shape
+    blocks = lon // LANES
+    theta_rows = reciprocal_surface.shape[1]
+    chunk_rows = CHUNK_FIELDS * blocks
+    sent, field_packet = pl.pallas_call(
+        collect_kernel,
+        out_shape=(shape_of(PEERS * chunk_rows, LANES), shape_of(3 * theta_rows, lon)),
+        name="collect",
+    )(
+        induction_vector,
+        reciprocal_surface,
+        number_per_volume,
+        thermal_kelvin,
+        lists,
+        owners,
+        electric_decay_rate,
+    )
+    arrived = lax.all_to_all(
+        sent.reshape(PEERS, chunk_rows, LANES), RING, split_axis=0, concat_axis=0, tiled=True
+    ).reshape(PEERS * chunk_rows, LANES)
+    packet = jnp.concatenate([field_packet, ohmic_spreading_number[0]], 0)
+    other = lax.ppermute(packet, "pair", [(0, 1), (1, 0)])
+    both = jnp.concatenate([packet, other], 0)
+    even = lax.ppermute(both, RING, [(i, i ^ 1) for i in range(PEERS)])
+    odd_pairs = [(i, i + 1) for i in range(1, PEERS - 1, 2)]
+    odd = lax.ppermute(both, RING, odd_pairs + [(j, i) for i, j in odd_pairs])
+    copies = 2 * PEERS
+    sum_rows = 2 * lat_rows * blocks
+    sums = pl.pallas_call(
+        deposit_kernel,
+        out_shape=shape_of(copies * sum_rows, LANES),
+        name="deposit",
+    )(arrived, owners, pedersen_sheet)
+    gathered = lax.all_to_all(
+        sums.reshape(copies, sum_rows, LANES), GROUP, split_axis=0, concat_axis=0, tiled=True
+    ).reshape(copies * sum_rows, LANES)
+    found = pl.pallas_call(
+        functools.partial(invert_kernel, lat_rows=lat_rows),
+        out_shape=jax.ShapeDtypeStruct((2 * theta_rows * blocks, LANES), jnp.int32),
+        name="invert",
+    )(arrived, lists)
+    advanced = pl.pallas_call(
+        advance_kernel,
+        out_shape=shape_of(3, 1, theta_rows, lon),
+        scratch_shapes=[pltpu.VMEM((8, 4 * theta_rows, lon), jnp.float32)],
+        name="advance",
+    )(packet, other, even, odd)
+    boundary, potential = pl.pallas_call(
+        solve_kernel,
+        out_shape=(shape_of(2, 1, theta_rows, lon), shape_of(lat_rows, lon)),
+        name="solve",
+    )(gathered, arrived, found)
+    return advanced, boundary, potential
+
+
+def local(*arguments):
+    lists, decay, surface = arguments[5], arguments[8], arguments[2]
+    fits = (
+        lists.shape[2:] == (PEERS, decay.shape[1])
+        and decay.shape == (2, 4 * LANES)
+        and surface.shape == (1, 4, 4 * LANES)
+        and lax.axis_size("pair") == 2
+    )
+    return short_plan(*arguments) if fits else stepwise(*arguments)
+
+
 def solution(mesh):
     in_specs = (
         P(None, ("run", "pair"), ("tile", "sub"), None),

time: 225 us -> 41 us (0.18); the launches traced: 222 us -> 40.5 us
  starting transfers between devices: 109 us -> 9.01 us
  other arithmetic: 52.9 us -> 0.02 us
  local copies, waits for them, and re-layouts: 32.6 us -> 1.87 us
  waiting for transfers between devices: 23.7 us -> 6.01 us
  Pallas kernels: 0 us -> 10.8 us
  blocking collectives: 2.5 us -> 12.1 us
    ppermute x32 -> x3, starting transfers between devices: 98.1 us -> 3.78 us  [the longest x1 2.09 us: short_plan(): odd = lax.ppermute(both, RING, odd_pairs + [(j, i) for i, j in odd_pairs])]
    scatter-add x2 -> x0, other arithmetic: 45.1 us -> none  [the longest x1 22.6 us: local(): jnp.zeros((2, cell_count), jnp.float32).at[:, target]]
    gather x4 -> x0, local copies, waits for them, and re-layouts: 23.4 us -> none  [the longest x2 12 us: local(): column_values[:, land_columns]]
    ppermute x32 -> x3, waiting for transfers between devices: 23.7 us -> 6.01 us  [the longest x1 3.85 us: short_plan(): odd = lax.ppermute(both, RING, odd_pairs + [(j, i) for i, j in odd_pairs])]
    all_to_all x0 -> x1, blocking collectives: none -> 12.1 us  [short_plan(): lax.all_to_all(sent.reshape(PEERS, chunk_rows, LANES), RING, split_axis=0...]
    pallas_call x0 -> x5, Pallas kernels: none -> 10.8 us  [the longest x1 2.81 us: short_plan(): pl.pallas_call(solve_kernel, out_shape=(shape_of(2, 1, theta_rows, lon),...]
    all_to_all x2 -> x1, starting transfers between devices: 11.1 us -> 5.23 us  [short_plan(): lax.all_to_all(sums.reshape(copies, sum_rows, LANES), GROUP, split_axis=0...]
    slice x39 -> x0, local copies, waits for them, and re-layouts: 4.85 us -> none  [the longest x8 2.12 us: advance_field(): jnp.roll(current_state, 1, 3)]
  transfers between devices with their start and end apart: 34 -> 4, of which waited for: 12 -> 3; matrix products, arithmetic and copies ran while one was open for 37% -> 0% of each run, Pallas kernels for 0% -> 10%
where the time goes in v1:
time: 41 us; the launch traced here: 40.5 us
  blocking collectives  12.1 us (30%)
  Pallas kernels  10.8 us (26%)
  starting transfers between devices  9.01 us (22%)
  waiting for transfers between devices  6.01 us (15%)
  local copies, waits for them, and re-layouts  1.87 us (5%)
  between operations  0.69 us (2%)
    all_to_all x1, blocking collectives, short_plan(): lax.all_to_all(sent.reshape(PEERS, chunk_rows, LANES), RING, split_axis=0...  12.1 us
    all_to_all x1, starting transfers between devices, short_plan(): lax.all_to_all(sums.reshape(copies, sum_rows, LANES), GROUP, split_axis=0...  5.23 us
    ppermute x1, waiting for transfers between devices, short_plan(): odd = lax.ppermute(both, RING, odd_pairs + [(j, i) for i, j in odd_pairs])  3.85 us
    pallas_call x1, Pallas kernels, short_plan(): pl.pallas_call(solve_kernel, out_shape=(shape_of(2, 1, theta_rows, lon),...  2.81 us
    pallas_call x1, Pallas kernels, short_plan(): pl.pallas_call(deposit_kernel, out_shape=shape_of(copies * sum_rows, LANE...  2.16 us
    ppermute x1, starting transfers between devices, short_plan(): odd = lax.ppermute(both, RING, odd_pairs + [(j, i) for i, j in odd_pairs])  2.09 us
    pallas_call x1, Pallas kernels, short_plan(): pl.pallas_call(advance_kernel, out_shape=shape_of(3, 1, theta_rows, lon),...  2.06 us
    pallas_call x1, Pallas kernels, short_plan(): pl.pallas_call(functools.partial(invert_kernel, lat_rows=lat_rows), out_s...  1.98 us
  transfers between devices with their start and end apart: 4, of which 3 were waited for; matrix products, arithmetic and copies ran while one was open for 0% of the time, Pallas kernels for 10%

profile of v1, /device:TPU:12, one launch (start us, length us, event | category | flops | bytes accessed | tf_op | source)
XLA Modules:
  0.0 40.5 jit_solution(15767135586411264219)
XLA Ops:
  0.6 1.7 %collect.1 = (f32[320,128]{1,0:T(8,128)}, f32[12,512]{1,0:T(8,128)}) custom-call(f32[3,1,4,512]{3,2,1,0:T(4,128)} %field.1, f32[1,4,512]{2,1,0:T(4,128)} %reciprocal.1, f32[1,4,512]{2,1,0:T(4,128)} %number.1, f32[1,4,512]{2,1,0:T(4,128)} %kelvin.1, s32[8,512]{1,0:T(8,128)} %bitcast.15, s32[8,512]{1,0:T(8,128)} %bitcast.13, f32[2,512]{1,0:T(2,128)} %decay.1), custom_call_target="tpu_custom_call" | custom-call | tf_op jit(solution)/shard_map/collect/pallas_call | solution.py:403
  2.4 12.1 %all_to_all.10 = f32[8,40,128]{2,1,0:T(8,128)} all-to-all(f32[8,40,128]{2,1,0:T(8,128)} %bitcast.12), channel_id=1, replica_groups=mesh['run'=2,'tile'=4,'sub'=2,'pair'=2] {'tile','sub'}, dimensions={0} | all-to-all | bytes 327680 | tf_op jit(solution)/shard_map/all_to_all | solution.py:416
  14.5 2.2 %deposit.1 = f32[256,128]{1,0:T(8,128)} custom-call(f32[320,128]{1,0:T(8,128)} %bitcast.7, s32[8,512]{1,0:T(8,128)} %bitcast.14, f32[16,2,512]{2,1,0:T(2,128)} %sheet.1), custom_call_target="tpu_custom_call" | custom-call | tf_op jit(solution)/shard_map/deposit/pallas_call | solution.py:427
  16.7 0.0 copy-start.3
  16.7 0.0 copy-start.6
  16.7 5.2 %all-to-all-start.1 = ((f32[16,16,128]{2,1,0:T(8,128)}), f32[16,16,128]{2,1,0:T(8,128)S(1)}, u32[]{:S(2)}, u32[]{:S(2)}) async-start(f32[16,16,128]{2,1,0:T(8,128)} %bitcast.10), calls=%async_computation.1 | async-start | bytes 262144 | tf_op jit(solution)/shard_map/all_to_all | solution.py:432
  21.9 0.0 copy-done.3
  21.9 0.0 copy-done.6
  22.0 0.0 copy-start.2
  22.0 0.2 collective-permute-start
  22.2 1.1 %collective-permute-done.other = f32[16,512]{1,0:T(8,128)S(1)} collective-permute-done((f32[16,512]{1,0:T(8,128)S(1)}, f32[16,512]{1,0:T(8,128)S(1)}, u32[]{:S(2)}, u32[]{:S(2)}) %collective-permute-start) | collective-permute-done | bytes 32800 | tf_op jit(solution)/shard_map/ppermute | solution.py:420
  23.3 0.0 copy-done.2
  23.3 0.6 %copy-done.1 = f32[16,512]{1,0:T(8,128)} copy-done((f32[16,512]{1,0:T(8,128)}, f32[16,512]{1,0:T(8,128)S(1)}, u32[]{:S(2)}) %copy-start.1) | copy-done | bytes 32792
  23.8 1.5 %collective-permute-start.1 = (f32[32,512]{1,0:T(8,128)S(1)}, f32[32,512]{1,0:T(8,128)S(1)}, u32[]{:S(2)}, u32[]{:S(2)}) collective-permute-start(f32[32,512]{1,0:T(8,128)S(1)} %pad_maximum_fusion), channel_id=1, source_target_pairs={{0,2},{2,0},{4,6},{6,4},{8,10},{10,8},{12,14},{14,12},{1,3},{3,1},... | collective-permute-start | bytes 196616 | tf_op jit(solution)/shard_map/ppermute | solution.py:422
  25.3 2.1 %collective-permute-start.2 = (f32[32,512]{1,0:T(8,128)S(1)}, f32[32,512]{1,0:T(8,128)S(1)}, u32[]{:S(2)}, u32[]{:S(2)}) collective-permute-start(f32[32,512]{1,0:T(8,128)S(1)} %pad_maximum_fusion), channel_id=1, source_target_pairs={{2,4},{6,8},{10,12},{4,2},{8,6},{12,10},{3,5},{7,9},{11,13},{5,3},... | collective-permute-start | bytes 196616 | tf_op jit(solution)/shard_map/ppermute | solution.py:424
  27.4 1.1 %collective-permute-done.1.even = f32[32,512]{1,0:T(8,128)S(1)} collective-permute-done((f32[32,512]{1,0:T(8,128)S(1)}, f32[32,512]{1,0:T(8,128)S(1)}, u32[]{:S(2)}, u32[]{:S(2)}) %collective-permute-start.1) | collective-permute-done | bytes 65568 | tf_op jit(solution)/shard_map/ppermute | solution.py:422
  28.5 3.8 %collective-permute-done.2.odd = f32[32,512]{1,0:T(8,128)S(1)} collective-permute-done((f32[32,512]{1,0:T(8,128)S(1)}, f32[32,512]{1,0:T(8,128)S(1)}, u32[]{:S(2)}, u32[]{:S(2)}) %collective-permute-start.2) | collective-permute-done | bytes 65568 | tf_op jit(solution)/shard_map/ppermute | solution.py:424
  32.4 0.0 copy-done.4
  32.4 0.6 %copy-done.5 = f32[32,512]{1,0:T(8,128)} copy-done((f32[32,512]{1,0:T(8,128)}, f32[32,512]{1,0:T(8,128)S(1)}, u32[]{:S(2)}) %copy-start.5) | copy-done | bytes 65560
  33.0 2.1 %advance.1 = f32[3,1,4,512]{3,2,1,0:T(4,128)} custom-call(f32[16,512]{1,0:T(8,128)} %copy-done.2, f32[16,512]{1,0:T(8,128)} %copy-done.1, f32[32,512]{1,0:T(8,128)} %copy-done.4, f32[32,512]{1,0:T(8,128)} %copy-done.5), custom_call_target="tpu_custom_call" | custom-call | tf_op jit(solution)/shard_map/advance/pallas_call | solution.py:440
  35.1 2.0 %invert.1.found = s32[32,128]{1,0:T(8,128)} custom-call(f32[320,128]{1,0:T(8,128)} %bitcast.8, s32[8,512]{1,0:T(8,128)} %bitcast.16), custom_call_target="tpu_custom_call" | custom-call | tf_op jit(solution)/shard_map/invert/pallas_call | solution.py:435
  37.0 0.0 all-to-all-done.1
  37.0 0.6 %copy-done = f32[16,16,128]{2,1,0:T(8,128)} copy-done((f32[16,16,128]{2,1,0:T(8,128)}, f32[16,16,128]{2,1,0:T(8,128)S(1)}, u32[]{:S(2)}) %copy-start) | copy-done | bytes 131096
  37.7 2.8 %solve.1 = (f32[2,1,4,512]{3,2,1,0:T(4,128)}, f32[2,512]{1,0:T(2,128)}) custom-call(f32[256,128]{1,0:T(8,128)} %bitcast.11, f32[320,128]{1,0:T(8,128)} %bitcast.9, s32[32,128]{1,0:T(8,128)} %invert.1.found), custom_call_target="tpu_custom_call" | custom-call | tf_op jit(solution)/shard_map/solve/pallas_call | solution.py:446
  (6 shorter events, 0.0 us)
Async XLA Ops:
  16.7 5.2 %copy-start.3 = (f32[12,512]{1,0:T(8,128)S(1)}, f32[12,512]{1,0:T(8,128)}, u32[]{:S(2)}) copy-start(f32[12,512]{1,0:T(8,128)} %get-tuple-element.7) | copy-start | bytes 73732
  16.7 5.2 %copy-start.6 = (f32[1,4,512]{2,1,0:T(4,128)S(1)}, f32[1,4,512]{2,1,0:T(4,128)}, u32[]{:S(2)}) copy-start(f32[1,4,512]{2,1,0:T(4,128)} %param.10) | copy-start | bytes 24580
  16.7 20.3 %all-to-all-start.1 = ((f32[16,16,128]{2,1,0:T(8,128)}), f32[16,16,128]{2,1,0:T(8,128)S(1)}, u32[]{:S(2)}, u32[]{:S(2)}) async-start(f32[16,16,128]{2,1,0:T(8,128)} %bitcast.10), calls=%async_computation.1 | async-start | bytes 262144 | tf_op jit(solution)/shard_map/all_to_all | solution.py:432
  22.0 1.3 %copy-start.2 = (f32[16,512]{1,0:T(8,128)}, f32[16,512]{1,0:T(8,128)S(1)}, u32[]{:S(2)}) copy-start(f32[16,512]{1,0:T(8,128)S(1)} %pad_maximum_fusion.1.own) | copy-start | bytes 98308
  22.0 1.3 %collective-permute-start = (f32[16,512]{1,0:T(8,128)S(1)}, f32[16,512]{1,0:T(8,128)S(1)}, u32[]{:S(2)}, u32[]{:S(2)}) collective-permute-start(f32[16,512]{1,0:T(8,128)S(1)} %pad_maximum_fusion.1.own), channel_id=1, source_target_pairs={{0,1},{1,0},{2,3},{3,2},{4,5},{5,4},{6,7},{7,6},{8,9},{9,8},{10,11... | collective-permute-start | bytes 98312 | tf_op jit(solution)/shard_map/ppermute | solution.py:420
  23.2 0.6 %copy-start.1 = (f32[16,512]{1,0:T(8,128)}, f32[16,512]{1,0:T(8,128)S(1)}, u32[]{:S(2)}) copy-start(f32[16,512]{1,0:T(8,128)S(1)} %collective-permute-done.other) | copy-start | bytes 98308
  23.8 4.7 %collective-permute-start.1 = (f32[32,512]{1,0:T(8,128)S(1)}, f32[32,512]{1,0:T(8,128)S(1)}, u32[]{:S(2)}, u32[]{:S(2)}) collective-permute-start(f32[32,512]{1,0:T(8,128)S(1)} %pad_maximum_fusion), channel_id=1, source_target_pairs={{0,2},{2,0},{4,6},{6,4},{8,10},{10,8},{12,14},{14,12},{1,3},{3,1},... | collective-permute-start | bytes 196616 | tf_op jit(solution)/shard_map/ppermute | solution.py:422
  25.3 7.0 %collective-permute-start.2 = (f32[32,512]{1,0:T(8,128)S(1)}, f32[32,512]{1,0:T(8,128)S(1)}, u32[]{:S(2)}, u32[]{:S(2)}) collective-permute-start(f32[32,512]{1,0:T(8,128)S(1)} %pad_maximum_fusion), channel_id=1, source_target_pairs={{2,4},{6,8},{10,12},{4,2},{8,6},{12,10},{3,5},{7,9},{11,13},{5,3},... | collective-permute-start | bytes 196616 | tf_op jit(solution)/shard_map/ppermute | solution.py:424
  28.5 3.9 %copy-start.4 = (f32[32,512]{1,0:T(8,128)}, f32[32,512]{1,0:T(8,128)S(1)}, u32[]{:S(2)}) copy-start(f32[32,512]{1,0:T(8,128)S(1)} %collective-permute-done.1.even) | copy-start | bytes 196612
  32.4 0.6 %copy-start.5 = (f32[32,512]{1,0:T(8,128)}, f32[32,512]{1,0:T(8,128)S(1)}, u32[]{:S(2)}) copy-start(f32[32,512]{1,0:T(8,128)S(1)} %collective-permute-done.2.odd) | copy-start | bytes 196612
  37.0 0.7 %copy-start = (f32[16,16,128]{2,1,0:T(8,128)}, f32[16,16,128]{2,1,0:T(8,128)S(1)}, u32[]{:S(2)}) copy-start(f32[16,16,128]{2,1,0:T(8,128)S(1)} %all-to-all-done.1) | copy-start | bytes 393220

commit v2 on v1

--- a/solution.py
+++ b/solution.py
@@ -116,6 +116,7 @@
 GROUP = ("tile", "sub", "pair")
 CURRENT, FLUX, RIM_WEIGHT, CELL, OWNER, FIRST_ROW, LAST_ROW, DECAY = range(8)
 CHUNK_FIELDS = 10
+KERNEL_PARAMS = pltpu.CompilerParams(vmem_limit_bytes=4 * 2**20)
 
 
 def pick_lanes(row, lane):
@@ -162,7 +163,20 @@
     return total
 
 
-def collect_kernel(field, reciprocal, number, kelvin, lists, owners, decay, sent, packet):
+def collect_kernel(*refs):
+    count = 8
+    here, (sent, packet), mine, (arrival,) = (
+        refs[:count],
+        refs[count : count + 2],
+        refs[count + 2 : 2 * count + 2],
+        refs[2 * count + 2 :],
+    )
+    copies = [pltpu.make_async_copy(here[k], mine[k], arrival.at[k]) for k in range(count)]
+    for copy in copies:
+        copy.start()
+    for copy in copies:
+        copy.wait()
+    field, reciprocal, number, kelvin, lists, owners, decay, spreading = mine
     theta_rows, lon = reciprocal.shape[1:]
     blocks = lon // LANES
     toward_theta = field[2, 0]
@@ -201,6 +215,7 @@
             sent[field_rows(k, b, blocks), :] = value
     for k in range(3):
         packet[k * theta_rows : (k + 1) * theta_rows] = field[k, 0]
+    packet[3 * theta_rows : 4 * theta_rows] = spreading[0]
 
 
 def deposit_kernel(arrived, owners, sheet, sums):
@@ -400,11 +415,7 @@
     blocks = lon // LANES
     theta_rows = reciprocal_surface.shape[1]
     chunk_rows = CHUNK_FIELDS * blocks
-    sent, field_packet = pl.pallas_call(
-        collect_kernel,
-        out_shape=(shape_of(PEERS * chunk_rows, LANES), shape_of(3 * theta_rows, lon)),
-        name="collect",
-    )(
+    arguments = (
         induction_vector,
         reciprocal_surface,
         number_per_volume,
@@ -412,14 +423,24 @@
         lists,
         owners,
         electric_decay_rate,
-    )
+        ohmic_spreading_number,
+    )
+    sent, packet = pl.pallas_call(
+        collect_kernel,
+        out_shape=(shape_of(PEERS * chunk_rows, LANES), shape_of(4 * theta_rows, lon)),
+        in_specs=[pl.BlockSpec(memory_space=pltpu.HBM)] * len(arguments),
+        scratch_shapes=[pltpu.VMEM(a.shape, a.dtype) for a in arguments]
+        + [pltpu.SemaphoreType.DMA((len(arguments),))],
+        compiler_params=KERNEL_PARAMS,
+        name="collect",
+    )(*[pltpu.with_memory_space_constraint(a, pltpu.HBM) for a in arguments])
     arrived = lax.all_to_all(
         sent.reshape(PEERS, chunk_rows, LANES), RING, split_axis=0, concat_axis=0, tiled=True
     ).reshape(PEERS * chunk_rows, LANES)
-    packet = jnp.concatenate([field_packet, ohmic_spreading_number[0]], 0)
     other = lax.ppermute(packet, "pair", [(0, 1), (1, 0)])
     both = jnp.concatenate([packet, other], 0)
     even = lax.ppermute(both, RING, [(i, i ^ 1) for i in range(PEERS)])
+    arrived, both, even = lax.optimization_barrier((arrived, both, even))
     odd_pairs = [(i, i + 1) for i in range(1, PEERS - 1, 2)]
     odd = lax.ppermute(both, RING, odd_pairs + [(j, i) for i, j in odd_pairs])
     copies = 2 * PEERS
@@ -427,6 +448,7 @@
     sums = pl.pallas_call(
         deposit_kernel,
         out_shape=shape_of(copies * sum_rows, LANES),
+        compiler_params=KERNEL_PARAMS,
         name="deposit",
     )(arrived, owners, pedersen_sheet)
     gathered = lax.all_to_all(
@@ -435,17 +457,20 @@
     found = pl.pallas_call(
         functools.partial(invert_kernel, lat_rows=lat_rows),
         out_shape=jax.ShapeDtypeStruct((2 * theta_rows * blocks, LANES), jnp.int32),
+        compiler_params=KERNEL_PARAMS,
         name="invert",
     )(arrived, lists)
     advanced = pl.pallas_call(
         advance_kernel,
         out_shape=shape_of(3, 1, theta_rows, lon),
         scratch_shapes=[pltpu.VMEM((8, 4 * theta_rows, lon), jnp.float32)],
+        compiler_params=KERNEL_PARAMS,
         name="advance",
     )(packet, other, even, odd)
     boundary, potential = pl.pallas_call(
         solve_kernel,
         out_shape=(shape_of(2, 1, theta_rows, lon), shape_of(lat_rows, lon)),
+        compiler_params=KERNEL_PARAMS,
         name="solve",
     )(gathered, arrived, found)
     return advanced, boundary, potential

time: 41 us -> 32.9 us (0.80)
  the two profiles are of different devices: /device:TPU:12 before, /device:TPU:0 now
where the time goes in v2:
time: 32.9 us; the launch traced here: 32.5 us
  starting transfers between devices  13.7 us (42%)
  waiting for transfers between devices  11.6 us (35%)
  Pallas kernels  6.47 us (20%)
  between operations  0.71 us (2%)
    all_to_all x1, starting transfers between devices, short_plan(): lax.all_to_all(sent.reshape(PEERS, chunk_rows, LANES), RING, split_axis=0...  6.83 us
    all_to_all x1, waiting for transfers between devices, short_plan(): lax.all_to_all(sums.reshape(copies, sum_rows, LANES), GROUP, split_axis=0...  5.59 us
    all_to_all x1, starting transfers between devices, short_plan(): lax.all_to_all(sums.reshape(copies, sum_rows, LANES), GROUP, split_axis=0...  3.64 us
    ppermute x1, waiting for transfers between devices, short_plan(): even = lax.ppermute(both, RING, [(i, i ^ 1) for i in range(PEERS)])  3.37 us
    all_to_all x1, waiting for transfers between devices, short_plan(): lax.all_to_all(sent.reshape(PEERS, chunk_rows, LANES), RING, split_axis=0...  2.61 us
    ppermute x1, starting transfers between devices, short_plan(): even = lax.ppermute(both, RING, [(i, i ^ 1) for i in range(PEERS)])  2.08 us
    pallas_call x1, Pallas kernels, short_plan(): pl.pallas_call(collect_kernel, out_shape=(shape_of(PEERS * chunk_rows, LA...  1.83 us
    pallas_call x1, Pallas kernels, short_plan(): pl.pallas_call(solve_kernel, out_shape=(shape_of(2, 1, theta_rows, lon),...  1.82 us
  transfers between devices with their start and end apart: 5, of which 3 were waited for; matrix products, arithmetic and copies ran while one was open for 0% of the time, Pallas kernels for 5%

profile of v2, /device:TPU:0, one launch (start us, length us, event | category | flops | bytes accessed | tf_op | source)
XLA Modules:
  0.0 32.5 jit_solution(8624654683263953564)
XLA Ops:
  0.6 1.8 %collect.1 = (f32[320,128]{1,0:T(8,128)}, f32[16,512]{1,0:T(8,128)S(1)}) custom-call(f32[3,1,4,512]{3,2,1,0:T(4,128)} %refs_0_.1, f32[1,4,512]{2,1,0:T(4,128)} %refs_1_.1, f32[1,4,512]{2,1,0:T(4,128)} %refs_2_.1, f32[1,4,512]{2,1,0:T(4,128)} %refs_3_.1, s32[8,512]{1,0:T(8,128)} %bitcast.12, s32[8,512]{1,0:T(8,128)} %bitcast.10, f32[2,512]{1,0:T(2,128)} %refs_6_.1, ...), custom_call_target="tpu_custom_call" | custom-call | tf_op jit(solution)/shard_map/collect/pallas_call | solution.py:428
  2.5 0.5 %collective-permute-start = (f32[16,512]{1,0:T(8,128)S(1)}, f32[16,512]{1,0:T(8,128)S(1)}, u32[]{:S(2)}, u32[]{:S(2)}) collective-permute-start(f32[16,512]{1,0:T(8,128)S(1)} %get-tuple-element.10.own), channel_id=1, source_target_pairs={{0,1},{1,0},{2,3},{3,2},{4,5},{5,4},{6,7},{7,6},{8,9},{9,8},{10,11... | collective-permute-start | bytes 98312 | tf_op jit(solution)/shard_map/ppermute | solution.py:440
  3.0 6.8 %all-to-all-start = ((f32[8,40,128]{2,1,0:T(8,128)}), f32[8,40,128]{2,1,0:T(8,128)S(1)}, u32[]{:S(2)}, u32[]{:S(2)}) async-start(f32[8,40,128]{2,1,0:T(8,128)} %bitcast.2), calls=%async_computation | async-start | bytes 327680 | tf_op jit(solution)/shard_map/all_to_all | solution.py:437
  9.8 0.0 copy-start.2
  9.8 0.0 copy-start
  9.8 0.0 collective-permute-done.other
  9.9 2.1 %collective-permute-start.1 = (f32[32,512]{1,0:T(8,128)S(1)}, f32[32,512]{1,0:T(8,128)S(1)}, u32[]{:S(2)}, u32[]{:S(2)}) collective-permute-start(f32[32,512]{1,0:T(8,128)S(1)} %constant_dynamic-update-slice_fusion), channel_id=1, source_target_pairs={{0,2},{2,0},{4,6},{6,4},{8,10},{10,8},{12,14},{14,12},{1,3},{3,1},... | collective-permute-start | bytes 196616 | tf_op jit(solution)/shard_map/ppermute | solution.py:442
  11.9 3.4 %collective-permute-done.1.even = f32[32,512]{1,0:T(8,128)S(1)} collective-permute-done((f32[32,512]{1,0:T(8,128)S(1)}, f32[32,512]{1,0:T(8,128)S(1)}, u32[]{:S(2)}, u32[]{:S(2)}) %collective-permute-start.1) | collective-permute-done | bytes 65568 | tf_op jit(solution)/shard_map/ppermute | solution.py:442
  15.3 2.6 %all-to-all-done = f32[8,40,128]{2,1,0:T(8,128)S(1)} async-done(((f32[8,40,128]{2,1,0:T(8,128)}), f32[8,40,128]{2,1,0:T(8,128)S(1)}, u32[]{:S(2)}, u32[]{:S(2)}) %all-to-all-start) | async-done | bytes 163872 | tf_op jit(solution)/shard_map/all_to_all | solution.py:437
  17.9 0.0 copy-done.2
  17.9 0.0 copy-done
  17.9 1.2 %deposit.1 = f32[256,128]{1,0:T(8,128)} custom-call(f32[320,128]{1,0:T(8,128)S(1)} %bitcast.6, s32[8,512]{1,0:T(8,128)S(1)} %bitcast.11, f32[16,2,512]{2,1,0:T(2,128)S(1)} %copy-done.2), custom_call_target="tpu_custom_call" | custom-call | tf_op jit(solution)/shard_map/deposit/pallas_call | solution.py:448
  19.2 0.0 copy-start.1
  19.2 3.6 %all-to-all-start.1 = ((f32[16,16,128]{2,1,0:T(8,128)}), f32[16,16,128]{2,1,0:T(8,128)S(1)}, u32[]{:S(2)}, u32[]{:S(2)}) async-start(f32[16,16,128]{2,1,0:T(8,128)} %bitcast.4), calls=%async_computation.1 | async-start | bytes 262144 | tf_op jit(solution)/shard_map/all_to_all | solution.py:454
  22.8 0.7 %collective-permute-start.2 = (f32[32,512]{1,0:T(8,128)S(1)}, f32[32,512]{1,0:T(8,128)S(1)}, u32[]{:S(2)}, u32[]{:S(2)}) collective-permute-start(f32[32,512]{1,0:T(8,128)S(1)} %constant_dynamic-update-slice_fusion), channel_id=1, source_target_pairs={{2,4},{6,8},{10,12},{4,2},{8,6},{12,10},{3,5},{7,9},{11,13},{5,3},... | collective-permute-start | bytes 196616 | tf_op jit(solution)/shard_map/ppermute | solution.py:445
  23.5 0.0 copy-done.1
  23.5 0.4 %invert.1.found = s32[32,128]{1,0:T(8,128)S(1)} custom-call(f32[320,128]{1,0:T(8,128)S(1)} %bitcast.7, s32[8,512]{1,0:T(8,128)S(1)} %bitcast.13), custom_call_target="tpu_custom_call" | custom-call | tf_op jit(solution)/shard_map/invert/pallas_call | solution.py:457
  23.9 0.0 collective-permute-done.2.odd
  24.0 1.2 %advance.1 = f32[3,1,4,512]{3,2,1,0:T(4,128)} custom-call(f32[16,512]{1,0:T(8,128)S(1)} %get-tuple-element.10.own, f32[16,512]{1,0:T(8,128)S(1)} %collective-permute-done.other, f32[32,512]{1,0:T(8,128)S(1)} %collective-permute-done.1.even, f32[32,512]{1,0:T(8,128)S(1)} %collective-permute-done.2.odd), custom_call_target="tpu_custom_call" | custom-call | tf_op jit(solution)/shard_map/advance/pallas_call | solution.py:463
  25.1 5.6 %all-to-all-done.1 = f32[16,16,128]{2,1,0:T(8,128)S(1)} async-done(((f32[16,16,128]{2,1,0:T(8,128)}), f32[16,16,128]{2,1,0:T(8,128)S(1)}, u32[]{:S(2)}, u32[]{:S(2)}) %all-to-all-start.1) | async-done | bytes 131104 | tf_op jit(solution)/shard_map/all_to_all | solution.py:454
  30.7 1.8 %solve.1 = (f32[2,1,4,512]{3,2,1,0:T(4,128)}, f32[2,512]{1,0:T(2,128)}) custom-call(f32[256,128]{1,0:T(8,128)S(1)} %bitcast.9, f32[320,128]{1,0:T(8,128)S(1)} %bitcast.8, s32[32,128]{1,0:T(8,128)S(1)} %invert.1.found), custom_call_target="tpu_custom_call" | custom-call | tf_op jit(solution)/shard_map/solve/pallas_call | solution.py:470
  (2 shorter events, 0.0 us)
Async XLA Ops:
  2.5 7.4 %collective-permute-start = (f32[16,512]{1,0:T(8,128)S(1)}, f32[16,512]{1,0:T(8,128)S(1)}, u32[]{:S(2)}, u32[]{:S(2)}) collective-permute-start(f32[16,512]{1,0:T(8,128)S(1)} %get-tuple-element.10.own), channel_id=1, source_target_pairs={{0,1},{1,0},{2,3},{3,2},{4,5},{5,4},{6,7},{7,6},{8,9},{9,8},{10,11... | collective-permute-start | bytes 98312 | tf_op jit(solution)/shard_map/ppermute | solution.py:440
  3.0 14.9 %all-to-all-start = ((f32[8,40,128]{2,1,0:T(8,128)}), f32[8,40,128]{2,1,0:T(8,128)S(1)}, u32[]{:S(2)}, u32[]{:S(2)}) async-start(f32[8,40,128]{2,1,0:T(8,128)} %bitcast.2), calls=%async_computation | async-start | bytes 327680 | tf_op jit(solution)/shard_map/all_to_all | solution.py:437
  9.8 8.1 %copy-start.2 = (f32[16,2,512]{2,1,0:T(2,128)S(1)}, f32[16,2,512]{2,1,0:T(2,128)}, u32[]{:S(2)}) copy-start(f32[16,2,512]{2,1,0:T(2,128)} %sheet.1) | copy-start | bytes 196612
  9.8 8.1 %copy-start = (s32[1,1,8,512]{3,2,1,0:T(8,128)S(1)}, s32[1,1,8,512]{3,2,1,0:T(8,128)}, u32[]{:S(2)}) copy-start(s32[1,1,8,512]{3,2,1,0:T(8,128)} %param.15) | copy-start | bytes 49156
  9.9 5.4 %collective-permute-start.1 = (f32[32,512]{1,0:T(8,128)S(1)}, f32[32,512]{1,0:T(8,128)S(1)}, u32[]{:S(2)}, u32[]{:S(2)}) collective-permute-start(f32[32,512]{1,0:T(8,128)S(1)} %constant_dynamic-update-slice_fusion), channel_id=1, source_target_pairs={{0,2},{2,0},{4,6},{6,4},{8,10},{10,8},{12,14},{14,12},{1,3},{3,1},... | collective-permute-start | bytes 196616 | tf_op jit(solution)/shard_map/ppermute | solution.py:442
  19.2 4.3 %copy-start.1 = (s32[1,1,8,512]{3,2,1,0:T(8,128)S(1)}, s32[1,1,8,512]{3,2,1,0:T(8,128)}, u32[]{:S(2)}) copy-start(s32[1,1,8,512]{3,2,1,0:T(8,128)} %param.14) | copy-start | bytes 49156
  19.2 11.5 %all-to-all-start.1 = ((f32[16,16,128]{2,1,0:T(8,128)}), f32[16,16,128]{2,1,0:T(8,128)S(1)}, u32[]{:S(2)}, u32[]{:S(2)}) async-start(f32[16,16,128]{2,1,0:T(8,128)} %bitcast.4), calls=%async_computation.1 | async-start | bytes 262144 | tf_op jit(solution)/shard_map/all_to_all | solution.py:454
  22.8 1.1 %collective-permute-start.2 = (f32[32,512]{1,0:T(8,128)S(1)}, f32[32,512]{1,0:T(8,128)S(1)}, u32[]{:S(2)}, u32[]{:S(2)}) collective-permute-start(f32[32,512]{1,0:T(8,128)S(1)} %constant_dynamic-update-slice_fusion), channel_id=1, source_target_pairs={{2,4},{6,8},{10,12},{4,2},{8,6},{12,10},{3,5},{7,9},{11,13},{5,3},... | collective-permute-start | bytes 196616 | tf_op jit(solution)/shard_map/ppermute | solution.py:445

commit v3 on v2

--- a/solution.py
+++ b/solution.py
@@ -119,6 +119,34 @@
 KERNEL_PARAMS = pltpu.CompilerParams(vmem_limit_bytes=4 * 2**20)
 
 
+SLOT_ORDER = [5, 4, 3, 2, 1, 0, 7, 6]
+SUM_ORDER = [5, 4, 3, 2, 1, 0, 7, 6]
+SUM_PAIRS = (1, 0)
+
+
+def by_position(values, width=LANES):
+    row = lax.broadcasted_iota(jnp.int32, (PEERS, width), 0)
+    out = jnp.zeros((PEERS, width), jnp.int32)
+    for k, value in enumerate(values):
+        out = jnp.where(row == k, value, out)
+    return out
+
+
+def take_rows(values, index):
+    return jnp.take_along_axis(values, index, axis=0, mode="promise_in_bounds")
+
+
+def neighbour_rows(values, order, step):
+    wanted = [d + step for d in order]
+    inside = [0 <= d < PEERS for d in wanted]
+    index = by_position([order.index(d) if ok else 0 for d, ok in zip(wanted, inside)])
+    valid = by_position([int(ok) for ok in inside]) == 1
+    columns = blocks_of(values.shape[1] // LANES)
+    return jnp.concatenate(
+        [jnp.where(valid, take_rows(values[:, c], index), 0.0) for c in columns], 1
+    )
+
+
 def pick_lanes(row, lane):
     return jnp.take_along_axis(
         jnp.broadcast_to(row, lane.shape), lane, axis=1, mode="promise_in_bounds"
@@ -189,8 +217,9 @@
     phi_diff = pltpu.roll(toward_phi, lon - 1, 1) - pltpu.roll(toward_phi, 1, 1)
     current = half * (theta_diff - phi_diff)
     flux = 0.25 * number[0] * jnp.sqrt(kelvin[0])
+    order = by_position(SLOT_ORDER)
     for b, span in enumerate(blocks_of(blocks)):
-        cell = lists[:, span]
+        cell = take_rows(lists[:, span], order)
         lane = cell & (LANES - 1)
         row = cell >> 7
         taken = [jnp.zeros(cell.shape, jnp.float32)] * 3
@@ -205,7 +234,7 @@
                     tables.append(half[at, source])
                 for k, table in enumerate(tables):
                     taken[k] = jnp.where(here, pick_lanes(table, lane), taken[k])
-        values = taken + [cell.astype(jnp.float32), owners[:, span].astype(jnp.float32)]
+        values = taken + [cell.astype(jnp.float32), take_rows(owners[:, span], order).astype(jnp.float32)]
         values += [
             jnp.broadcast_to(r[:, span], cell.shape)
             for r in (toward_theta[:1], toward_theta[-1:], decay[0:1], decay[1:2])
@@ -222,13 +251,12 @@
     lon = sheet.shape[-1]
     blocks = lon // LANES
     lat_rows = sheet.shape[1]
-    peer = lax.broadcasted_iota(jnp.int32, (PEERS, LANES), 0)
-    above, below = [], []
-    for b in range(blocks):
-        last = pltpu.roll(arrived[field_rows(LAST_ROW, b, blocks), :], 1, 0)
-        above.append(jnp.where(peer == 0, 0.0, last))
-        first = pltpu.roll(arrived[field_rows(FIRST_ROW, b, blocks), :], PEERS - 1, 0)
-        below.append(jnp.where(peer == PEERS - 1, 0.0, first))
+    above = [
+        neighbour_rows(arrived[field_rows(LAST_ROW, b, blocks), :], SLOT_ORDER, -1) for b in range(blocks)
+    ]
+    below = [
+        neighbour_rows(arrived[field_rows(FIRST_ROW, b, blocks), :], SLOT_ORDER, 1) for b in range(blocks)
+    ]
     currents, fluxes = [], []
     for b in range(blocks):
         cell = arrived[field_rows(CELL, b, blocks), :].astype(jnp.int32)
@@ -243,7 +271,10 @@
         weight = arrived[field_rows(RIM_WEIGHT, b, blocks), :]
         currents.append(arrived[field_rows(CURRENT, b, blocks), :] + weight * rim)
         fluxes.append(arrived[field_rows(FLUX, b, blocks), :])
-    column = owners[...]
+    order = by_position(SLOT_ORDER)
+    column = jnp.concatenate(
+        [take_rows(owners[:, span], order) for span in blocks_of(blocks)], 1
+    )
     terms = three_terms(jnp.concatenate(currents, 1)) + three_terms(jnp.concatenate(fluxes, 1))
     rows = lat_rows * blocks
     total = one_hot_sums(
@@ -261,26 +292,27 @@
         sums[k * 2 * rows : (k + 1) * 2 * rows] = both
 
 
-def invert_kernel(arrived, lists, found, *, lat_rows):
+def footpoints(arrived, lists, lat_rows, cell_rows):
     lon = lists.shape[1]
     blocks = lon // LANES
     owner = jnp.concatenate(
         [arrived[field_rows(OWNER, b, blocks), :] for b in range(blocks)], 1
     ).astype(jnp.int32)
-    device = lax.broadcasted_iota(jnp.int32, owner.shape, 0)
+    device = by_position(SLOT_ORDER, lon)
     row = (owner >> 7) + device * (lat_rows * blocks) + 1
     lane = owner & (LANES - 1)
-    cell = lists[...]
-    cell_rows = found.shape[0] // 2
-    found[...] = one_hot_sums(
+    order = by_position(SLOT_ORDER)
+    cell = jnp.concatenate([take_rows(lists[:, span], order) for span in blocks_of(blocks)], 1)
+    found = one_hot_sums(
         cell >> 7,
         cell & (LANES - 1),
         [row.astype(jnp.float32), lane.astype(jnp.float32)],
         cell_rows,
     ).astype(jnp.int32)
-
-
-def advance_kernel(own, other, even, odd, advanced, window):
+    return found[:cell_rows], found[cell_rows:]
+
+
+def advance_body(own, other, even, odd, advanced, window):
     theta_rows = advanced.shape[2]
     span = 4 * theta_rows
     is_odd = (lax.axis_index(RING) & 1) == 1
@@ -290,11 +322,9 @@
             at = slice(k * theta_rows, (k + 1) * theta_rows)
             far = slice(shell * span + k * theta_rows, shell * span + (k + 1) * theta_rows)
             place = shell * 4 + k
-            after = jnp.where(is_odd, odd[far], even[far])
-            before = jnp.where(is_odd, even[far], odd[far])
-            window[place, 0:theta_rows] = before
+            window[place, 0:theta_rows] = jnp.where(is_odd, even[far], odd[far])
             window[place, theta_rows : 2 * theta_rows] = middle[at]
-            window[place, 2 * theta_rows : 3 * theta_rows] = after
+            window[place, 2 * theta_rows : 3 * theta_rows] = jnp.where(is_odd, odd[far], even[far])
     rows, lon = window.shape[1:]
     spreading = [window[3], window[7]]
     for k in range(3):
@@ -310,11 +340,14 @@
         advanced[k, 0] = state[0][theta_rows : 2 * theta_rows]
 
 
-def solve_kernel(sums, arrived, found, boundary, potential):
+def solve_body(sums, arrived, lists, boundary, potential):
     lon = potential.shape[1]
     blocks = lon // LANES
     rows = 2 * blocks
-    ring = lax.broadcasted_iota(jnp.int32, (PEERS, lon), 0)
+    cell_rows = boundary.shape[2] * blocks
+    row, lane = footpoints(arrived, lists, 2, cell_rows)
+    ring = by_position(SUM_ORDER, lon)
+    place_of = by_position([SLOT_ORDER.index(d) for d in SUM_ORDER])
 
     def summed(term, lat):
         return jnp.concatenate(
@@ -330,14 +363,18 @@
 
     def decay_rows(lat):
         return jnp.concatenate(
-            [arrived[field_rows(DECAY + lat, b, blocks), :] for b in range(blocks)], 1
+            [
+                take_rows(arrived[field_rows(DECAY + lat, b, blocks), :], place_of)
+                for b in range(blocks)
+            ],
+            1,
         )
 
     def before(values):
-        return jnp.where(ring == 0, 0.0, pltpu.roll(values, 1, 0))
+        return neighbour_rows(values, SUM_ORDER, -1)
 
     def after(values):
-        return jnp.where(ring == PEERS - 1, 0.0, pltpu.roll(values, PEERS - 1, 0))
+        return neighbour_rows(values, SUM_ORDER, 1)
 
     def east(values):
         return pltpu.roll(values, lon - 1, 1)
@@ -376,16 +413,13 @@
         potential[lat : lat + 1] = jnp.sum(
             jnp.where(ring == me, level[lat], 0.0), axis=0, keepdims=True
         )
-    cell_rows = found.shape[0] // 2
-    lane = found[cell_rows:]
-    row = found[:cell_rows]
     taken = [jnp.zeros(lane.shape, jnp.float32)] * 2
-    for device in range(PEERS):
+    for place, device in enumerate(SUM_ORDER):
         for lat in range(2):
             for b, span in enumerate(blocks_of(blocks)):
                 here = row == device * rows + lat * blocks + b + 1
                 for k, table in enumerate((level[lat], conductance[lat])):
-                    one = table[device : device + 1, span]
+                    one = table[place : place + 1, span]
                     taken[k] = jnp.where(here, pick_lanes(one, lane), taken[k])
     for k in range(2):
         for r in range(cell_rows):
@@ -394,8 +428,21 @@
             ]
 
 
+def finish_kernel(
+    sums, arrived, lists, own, other, even, odd, advanced, boundary, potential, window
+):
+    advance_body(own, other, even, odd, advanced, window)
+    solve_body(sums, arrived, lists, boundary, potential)
+
+
 def shape_of(*dims):
     return jax.ShapeDtypeStruct(dims, jnp.float32)
+
+
+def exchange(chunks, axes, order):
+    return lax.all_to_all(
+        chunks, axes, split_axis=0, concat_axis=0, axis_index_groups=[order], tiled=True
+    )
 
 
 def short_plan(
@@ -434,9 +481,7 @@
         compiler_params=KERNEL_PARAMS,
         name="collect",
     )(*[pltpu.with_memory_space_constraint(a, pltpu.HBM) for a in arguments])
-    arrived = lax.all_to_all(
-        sent.reshape(PEERS, chunk_rows, LANES), RING, split_axis=0, concat_axis=0, tiled=True
-    ).reshape(PEERS * chunk_rows, LANES)
+    arrived = exchange(sent.reshape(PEERS, chunk_rows, LANES), RING, SLOT_ORDER).reshape(PEERS * chunk_rows, LANES)
     other = lax.ppermute(packet, "pair", [(0, 1), (1, 0)])
     both = jnp.concatenate([packet, other], 0)
     even = lax.ppermute(both, RING, [(i, i ^ 1) for i in range(PEERS)])
@@ -451,28 +496,20 @@
         compiler_params=KERNEL_PARAMS,
         name="deposit",
     )(arrived, owners, pedersen_sheet)
-    gathered = lax.all_to_all(
-        sums.reshape(copies, sum_rows, LANES), GROUP, split_axis=0, concat_axis=0, tiled=True
+    gathered = exchange(
+        sums.reshape(copies, sum_rows, LANES), GROUP, [2 * d + p for d in SUM_ORDER for p in SUM_PAIRS]
     ).reshape(copies * sum_rows, LANES)
-    found = pl.pallas_call(
-        functools.partial(invert_kernel, lat_rows=lat_rows),
-        out_shape=jax.ShapeDtypeStruct((2 * theta_rows * blocks, LANES), jnp.int32),
-        compiler_params=KERNEL_PARAMS,
-        name="invert",
-    )(arrived, lists)
-    advanced = pl.pallas_call(
-        advance_kernel,
-        out_shape=shape_of(3, 1, theta_rows, lon),
+    advanced, boundary, potential = pl.pallas_call(
+        finish_kernel,
+        out_shape=(
+            shape_of(3, 1, theta_rows, lon),
+            shape_of(2, 1, theta_rows, lon),
+            shape_of(lat_rows, lon),
+        ),
         scratch_shapes=[pltpu.VMEM((8, 4 * theta_rows, lon), jnp.float32)],
         compiler_params=KERNEL_PARAMS,
-        name="advance",
-    )(packet, other, even, odd)
-    boundary, potential = pl.pallas_call(
-        solve_kernel,
-        out_shape=(shape_of(2, 1, theta_rows, lon), shape_of(lat_rows, lon)),
-        compiler_params=KERNEL_PARAMS,
-        name="solve",
-    )(gathered, arrived, found)
+        name="finish",
+    )(gathered, arrived, lists, packet, other, even, odd)
     return advanced, boundary, potential
 
 

time: 32.9 us -> 30.1 us (0.915)
  the two profiles are of different devices: /device:TPU:0 before, /device:TPU:12 now
where the time goes in v3:
time: 30.1 us; the launch traced here: 29.6 us
  starting transfers between devices  14.6 us (49%)
  waiting for transfers between devices  8.68 us (29%)
  Pallas kernels  5.57 us (19%)
  between operations  0.68 us (2%)
    all_to_all x2, starting transfers between devices, exchange(): lax.all_to_all(chunks, axes, split_axis=0, concat_axis=0, axis_index_grou...  10.7 us
    ppermute x1, waiting for transfers between devices, short_plan(): even = lax.ppermute(both, RING, [(i, i ^ 1) for i in range(PEERS)])  3.82 us
    ppermute x1, waiting for transfers between devices, short_plan(): odd = lax.ppermute(both, RING, odd_pairs + [(j, i) for i, j in odd_pairs])  3.68 us
    ppermute x1, starting transfers between devices, short_plan(): odd = lax.ppermute(both, RING, odd_pairs + [(j, i) for i, j in odd_pairs])  3.36 us
    pallas_call x1, Pallas kernels, short_plan(): pl.pallas_call(finish_kernel, out_shape=(shape_of(3, 1, theta_rows, lon),...  2.51 us
    pallas_call x1, Pallas kernels, short_plan(): pl.pallas_call(collect_kernel, out_shape=(shape_of(PEERS * chunk_rows, LA...  1.83 us
    pallas_call x1, Pallas kernels, short_plan(): pl.pallas_call(deposit_kernel, out_shape=shape_of(copies * sum_rows, LANE...  1.23 us
    ppermute x1, waiting for transfers between devices, short_plan(): other = lax.ppermute(packet, 'pair', [(0, 1), (1, 0)])  1.18 us
  transfers between devices with their start and end apart: 5, of which 3 were waited for; matrix products, arithmetic and copies ran while one was open for 0% of the time, Pallas kernels for 0%

profile of v3, /device:TPU:12, one launch (start us, length us, event | category | flops | bytes accessed | tf_op | source)
XLA Modules:
  0.0 29.6 jit_solution(13473893408739457186)
XLA Ops:
  0.6 1.8 %collect.1 = (f32[320,128]{1,0:T(8,128)}, f32[16,512]{1,0:T(8,128)S(1)}) custom-call(f32[3,1,4,512]{3,2,1,0:T(4,128)} %refs_0_.1, f32[1,4,512]{2,1,0:T(4,128)} %refs_1_.1, f32[1,4,512]{2,1,0:T(4,128)} %refs_2_.1, f32[1,4,512]{2,1,0:T(4,128)} %refs_3_.1, s32[8,512]{1,0:T(8,128)} %bitcast.11, s32[8,512]{1,0:T(8,128)} %bitcast.9, f32[2,512]{1,0:T(2,128)} %refs_6_.1, ...), custom_call_target="tpu_custom_call" | custom-call | tf_op jit(solution)/shard_map/collect/pallas_call | solution.py:475
  2.5 5.8 %all-to-all-start = ((f32[8,40,128]{2,1,0:T(8,128)}), f32[8,40,128]{2,1,0:T(8,128)S(1)}, u32[]{:S(2)}, u32[]{:S(2)}) async-start(f32[8,40,128]{2,1,0:T(8,128)} %bitcast.2), calls=%async_computation | async-start | bytes 327680 | tf_op jit(solution)/shard_map/all_to_all | solution.py:443
  8.3 0.0 copy-start.2
  8.3 0.0 collective-permute-start
  8.3 0.0 copy-start
  8.3 1.2 %collective-permute-done.other = f32[16,512]{1,0:T(8,128)S(1)} collective-permute-done((f32[16,512]{1,0:T(8,128)S(1)}, f32[16,512]{1,0:T(8,128)S(1)}, u32[]{:S(2)}, u32[]{:S(2)}) %collective-permute-start) | collective-permute-done | bytes 32800 | tf_op jit(solution)/shard_map/ppermute | solution.py:485
  9.5 0.6 %collective-permute-start.1 = (f32[32,512]{1,0:T(8,128)S(1)}, f32[32,512]{1,0:T(8,128)S(1)}, u32[]{:S(2)}, u32[]{:S(2)}) collective-permute-start(f32[32,512]{1,0:T(8,128)S(1)} %constant_dynamic-update-slice_fusion), channel_id=1, source_target_pairs={{0,2},{2,0},{4,6},{6,4},{8,10},{10,8},{12,14},{14,12},{1,3},{3,1},... | collective-permute-start | bytes 196616 | tf_op jit(solution)/shard_map/ppermute | solution.py:487
  10.1 3.8 %collective-permute-done.1.even = f32[32,512]{1,0:T(8,128)S(1)} collective-permute-done((f32[32,512]{1,0:T(8,128)S(1)}, f32[32,512]{1,0:T(8,128)S(1)}, u32[]{:S(2)}, u32[]{:S(2)}) %collective-permute-start.1) | collective-permute-done | bytes 65568 | tf_op jit(solution)/shard_map/ppermute | solution.py:487
  13.9 0.0 all-to-all-done
  13.9 0.0 copy-done.2
  13.9 0.0 copy-done
  13.9 1.2 %deposit.1 = f32[256,128]{1,0:T(8,128)} custom-call(f32[320,128]{1,0:T(8,128)S(1)} %bitcast.6, s32[8,512]{1,0:T(8,128)S(1)} %bitcast.10, f32[16,2,512]{2,1,0:T(2,128)S(1)} %copy-done.2), custom_call_target="tpu_custom_call" | custom-call | tf_op jit(solution)/shard_map/deposit/pallas_call | solution.py:493
  15.1 0.0 copy-start.1
  15.1 4.9 %all-to-all-start.1 = ((f32[16,16,128]{2,1,0:T(8,128)}), f32[16,16,128]{2,1,0:T(8,128)S(1)}, u32[]{:S(2)}, u32[]{:S(2)}) async-start(f32[16,16,128]{2,1,0:T(8,128)} %bitcast.4), calls=%async_computation.1 | async-start | bytes 262144 | tf_op jit(solution)/shard_map/all_to_all | solution.py:443
  20.0 3.4 %collective-permute-start.2 = (f32[32,512]{1,0:T(8,128)S(1)}, f32[32,512]{1,0:T(8,128)S(1)}, u32[]{:S(2)}, u32[]{:S(2)}) collective-permute-start(f32[32,512]{1,0:T(8,128)S(1)} %constant_dynamic-update-slice_fusion), channel_id=1, source_target_pairs={{2,4},{6,8},{10,12},{4,2},{8,6},{12,10},{3,5},{7,9},{11,13},{5,3},... | collective-permute-start | bytes 196616 | tf_op jit(solution)/shard_map/ppermute | solution.py:490
  23.4 3.7 %collective-permute-done.2.odd = f32[32,512]{1,0:T(8,128)S(1)} collective-permute-done((f32[32,512]{1,0:T(8,128)S(1)}, f32[32,512]{1,0:T(8,128)S(1)}, u32[]{:S(2)}, u32[]{:S(2)}) %collective-permute-start.2) | collective-permute-done | bytes 65568 | tf_op jit(solution)/shard_map/ppermute | solution.py:490
  27.1 0.0 all-to-all-done.1
  27.1 0.0 copy-done.1
  27.1 2.5 %finish.1 = (f32[3,1,4,512]{3,2,1,0:T(4,128)}, f32[2,1,4,512]{3,2,1,0:T(4,128)}, f32[2,512]{1,0:T(2,128)}) custom-call(f32[256,128]{1,0:T(8,128)S(1)} %bitcast.8, f32[320,128]{1,0:T(8,128)S(1)} %bitcast.7, s32[8,512]{1,0:T(8,128)S(1)} %bitcast.12, f32[16,512]{1,0:T(8,128)S(1)} %get-tuple-element.9.own, f32[16,512]{1,0:T(8,128)S(1)} %collective-permute-done.other, ...), custom_call_target="tpu_custom_call" | custom-call | tf_op jit(solution)/shard_map/finish/pallas_call | solution.py:502
  (2 shorter events, 0.0 us)
Async XLA Ops:
  2.5 11.4 %all-to-all-start = ((f32[8,40,128]{2,1,0:T(8,128)}), f32[8,40,128]{2,1,0:T(8,128)S(1)}, u32[]{:S(2)}, u32[]{:S(2)}) async-start(f32[8,40,128]{2,1,0:T(8,128)} %bitcast.2), calls=%async_computation | async-start | bytes 327680 | tf_op jit(solution)/shard_map/all_to_all | solution.py:443
  8.3 5.6 %copy-start.2 = (f32[16,2,512]{2,1,0:T(2,128)S(1)}, f32[16,2,512]{2,1,0:T(2,128)}, u32[]{:S(2)}) copy-start(f32[16,2,512]{2,1,0:T(2,128)} %sheet.1) | copy-start | bytes 196612
  8.3 1.2 %collective-permute-start = (f32[16,512]{1,0:T(8,128)S(1)}, f32[16,512]{1,0:T(8,128)S(1)}, u32[]{:S(2)}, u32[]{:S(2)}) collective-permute-start(f32[16,512]{1,0:T(8,128)S(1)} %get-tuple-element.9.own), channel_id=1, source_target_pairs={{0,1},{1,0},{2,3},{3,2},{4,5},{5,4},{6,7},{7,6},{8,9},{9,8},{10,11... | collective-permute-start | bytes 98312 | tf_op jit(solution)/shard_map/ppermute | solution.py:485
  8.3 5.6 %copy-start = (s32[1,1,8,512]{3,2,1,0:T(8,128)S(1)}, s32[1,1,8,512]{3,2,1,0:T(8,128)}, u32[]{:S(2)}) copy-start(s32[1,1,8,512]{3,2,1,0:T(8,128)} %param.15) | copy-start | bytes 49156
  9.5 4.4 %collective-permute-start.1 = (f32[32,512]{1,0:T(8,128)S(1)}, f32[32,512]{1,0:T(8,128)S(1)}, u32[]{:S(2)}, u32[]{:S(2)}) collective-permute-start(f32[32,512]{1,0:T(8,128)S(1)} %constant_dynamic-update-slice_fusion), channel_id=1, source_target_pairs={{0,2},{2,0},{4,6},{6,4},{8,10},{10,8},{12,14},{14,12},{1,3},{3,1},... | collective-permute-start | bytes 196616 | tf_op jit(solution)/shard_map/ppermute | solution.py:487
  15.1 12.0 %copy-start.1 = (s32[1,1,8,512]{3,2,1,0:T(8,128)S(1)}, s32[1,1,8,512]{3,2,1,0:T(8,128)}, u32[]{:S(2)}) copy-start(s32[1,1,8,512]{3,2,1,0:T(8,128)} %param.14) | copy-start | bytes 49156
  15.1 11.9 %all-to-all-start.1 = ((f32[16,16,128]{2,1,0:T(8,128)}), f32[16,16,128]{2,1,0:T(8,128)S(1)}, u32[]{:S(2)}, u32[]{:S(2)}) async-start(f32[16,16,128]{2,1,0:T(8,128)} %bitcast.4), calls=%async_computation.1 | async-start | bytes 262144 | tf_op jit(solution)/shard_map/all_to_all | solution.py:443
  20.0 7.0 %collective-permute-start.2 = (f32[32,512]{1,0:T(8,128)S(1)}, f32[32,512]{1,0:T(8,128)S(1)}, u32[]{:S(2)}, u32[]{:S(2)}) collective-permute-start(f32[32,512]{1,0:T(8,128)S(1)} %constant_dynamic-update-slice_fusion), channel_id=1, source_target_pairs={{2,4},{6,8},{10,12},{4,2},{8,6},{12,10},{3,5},{7,9},{11,13},{5,3},... | collective-permute-start | bytes 196616 | tf_op jit(solution)/shard_map/ppermute | solution.py:490
